TPU v7x, 1024 devices: a whole 4x8x16 slice. The times are simulated.
1024 devices in a mesh: rep: 64 (over y, x, core), ep: 16 (over z).
Axes of the slice: x: 4, y: 8, z: 16, core: 2. Of those that a mesh axis runs over, the one named last changes fastest.
Arguments:
- tokens: bfloat16 [131072, 2048], P(('rep', 'ep')), may hold values from -6 to 6
- expert_ids: int32 [131072, 1], P(('rep', 'ep')), may hold values from 0 to 15; in each aligned block of 128 rows (0 to 127, 128 to 255, ...) at most 12 rows name the same one
- gate_weights: float32 [131072, 1], P(('rep', 'ep')), may hold values from 0.2 to 1
- cotangent: bfloat16 [131072, 2048], P(('rep', 'ep')), may hold values from -6 to 6
- gate_weight: bfloat16 [16, 2048, 384], P('ep'), may hold values from -0.125 to 0.125
- up_weight: bfloat16 [16, 2048, 384], P('ep'), may hold values from -0.125 to 0.125
- down_weight: bfloat16 [16, 384, 2048], P('ep'), may hold values from -0.3125 to 0.3125
Outputs:
- layer_out: bfloat16 [131072, 2048], P(('rep', 'ep'))
- token_grad: bfloat16 [131072, 2048], P(('rep', 'ep'))
- gate_grad: float32 [131072, 1], P(('rep', 'ep'))
- down_grad: float32 [16, 384, 2048], P('ep', 'rep')
Inputs may be any that keep to these rules, and one draw needn't show every extreme that they name: `expert_ids`: each token names 1 different experts. Among the rows of one device, at most 12 name the same expert, and in some devices' rows one expert is named by exactly 12.
All inputs are finite; a program needn't handle non-finite values.
Results may differ from a plain program's by a relative error of at most 0.0058.
Values may be sent and summed in bfloat16 or wider, within the bound.
A program may use at most 64 MiB of HBM per device.

v0:
```python
import jax
import jax.numpy as jnp
from jax import lax
from jax.sharding import PartitionSpec as P


def group_grad(hidden, recv_grad):
    return jnp.einsum("secf,secd->efd", hidden, recv_grad, preferred_element_type=jnp.float32)


def shards(tokens, expert_ids, gate_weights, cotangent, gate_weight, up_weight, down_weight):
    tok_rows = tokens.shape[0]
    model_width = tokens.shape[1]
    topk_count = expert_ids.shape[1]
    ep_size = lax.axis_size("ep")
    local_experts = gate_weight.shape[0]
    experts_all = local_experts * ep_size
    route_rows = tok_rows * topk_count
    capacity = 3 * route_rows // (2 * experts_all)
    flat_ids = expert_ids.reshape(route_rows)
    onehot = (flat_ids[:, None] == jnp.arange(experts_all, dtype=jnp.int32)[None, :]).astype(
        jnp.int32
    )
    earlier = jnp.cumsum(onehot, axis=0) - onehot
    slot_index = jnp.sum(earlier * onehot, axis=1)
    target = flat_ids * capacity + slot_index
    placing = (
        target[None, :] == jnp.arange(experts_all * capacity, dtype=jnp.int32)[:, None]
    ).astype(jnp.bfloat16)
    token_rows = jnp.repeat(tokens, topk_count, axis=0)
    cot_rows = jnp.repeat(cotangent, topk_count, axis=0)
    dout_rows = (gate_weights * cot_rows.astype(jnp.float32)).astype(jnp.bfloat16)
    block_shape = (ep_size, local_experts, capacity, model_width)
    send_rows = (
        jnp.dot(placing, token_rows, preferred_element_type=jnp.float32)
        .astype(jnp.bfloat16)
        .reshape(block_shape)
    )
    send_grad = (
        jnp.dot(placing, dout_rows, preferred_element_type=jnp.float32)
        .astype(jnp.bfloat16)
        .reshape(block_shape)
    )
    recv_rows, recv_grad = (
        lax.all_to_all(send_rows, "ep", split_axis=0, concat_axis=0, tiled=True),
        lax.all_to_all(send_grad, "ep", split_axis=0, concat_axis=0, tiled=True),
    )
    gate_pre = jnp.einsum(
        "secd,edf->secf", recv_rows, gate_weight, preferred_element_type=jnp.float32
    )
    up_pre = jnp.einsum("secd,edf->secf", recv_rows, up_weight, preferred_element_type=jnp.float32)
    gate_act = jax.nn.silu(gate_pre)
    hidden = (gate_act * up_pre).astype(jnp.bfloat16)
    expert_out = jnp.einsum(
        "secf,efd->secd", hidden, down_weight, preferred_element_type=jnp.float32
    ).astype(jnp.bfloat16)
    hidden_grad = jnp.einsum(
        "secd,efd->secf", recv_grad, down_weight, preferred_element_type=jnp.float32
    )
    sigma = jax.nn.sigmoid(gate_pre)
    gate_back = (hidden_grad * up_pre * sigma * (1.0 + gate_pre * (1.0 - sigma))).astype(
        jnp.bfloat16
    )
    up_back = (hidden_grad * gate_act).astype(jnp.bfloat16)
    input_back = (
        jnp.einsum("secf,edf->secd", gate_back, gate_weight, preferred_element_type=jnp.float32)
        + jnp.einsum("secf,edf->secd", up_back, up_weight, preferred_element_type=jnp.float32)
    ).astype(jnp.bfloat16)
    down_grad = lax.psum_scatter(
        group_grad(hidden, recv_grad), "rep", scatter_dimension=1, tiled=True
    )
    ret_out, ret_back = (
        lax.all_to_all(expert_out, "ep", split_axis=0, concat_axis=0, tiled=True),
        lax.all_to_all(input_back, "ep", split_axis=0, concat_axis=0, tiled=True),
    )
    flat_out = ret_out.reshape(experts_all * capacity, model_width)
    flat_back = ret_back.reshape(experts_all * capacity, model_width)
    contract = (((0,), (0,)), ((), ()))
    back_out = lax.dot_general(placing, flat_out, contract, preferred_element_type=jnp.float32)
    back_in = lax.dot_general(placing, flat_back, contract, preferred_element_type=jnp.float32)
    layer_out = jnp.sum(
        (gate_weights * back_out).reshape(tok_rows, topk_count, model_width), axis=1
    ).astype(jnp.bfloat16)
    gate_grad = jnp.sum(cot_rows.astype(jnp.float32) * back_out, axis=1).reshape(
        tok_rows, topk_count
    )
    token_grad = jnp.sum(back_in.reshape(tok_rows, topk_count, model_width), axis=1).astype(
        jnp.bfloat16
    )
    return (layer_out, token_grad, gate_grad, down_grad)


def solution(mesh):
    placed = (
        P(("rep", "ep"), None),
        P(("rep", "ep"), None),
        P(("rep", "ep"), None),
        P(("rep", "ep"), None),
        P("ep", None, None),
        P("ep", None, None),
        P("ep", None, None),
    )
    return jax.shard_map(
        shards,
        mesh=mesh,
        in_specs=placed,
        out_specs=(
            P(("rep", "ep"), None),
            P(("rep", "ep"), None),
            P(("rep", "ep"), None),
            P("ep", "rep", None),
        ),
        check_vma=False,
    )
```

profile of v0, /device:TPU:1, one launch (start us, length us, event | category | flops | bytes accessed | tf_op | source)
XLA Modules:
  0.0 457.7 jit_solution(1301378699855016880)
XLA Ops:
  7.2 0.0 copy-start
  7.2 0.9 fusion.40
  8.0 0.2 reduce_window_sum.11
  8.2 0.8 select_reduce_fusion
  9.0 0.7 multiply_add_fusion
  9.7 1.4 convolution_convert_fusion.1
  11.1 0.0 copy-start.1
  11.1 0.0 copy-start.6
  11.1 1.2 reshape.81
  12.3 19.5 %all-to-all-start = ((bf16[16,1,12,2048]{3,2,1,0:T(8,128)(2,1)}), bf16[16,1,12,2048]{3,2,1,0:T(8,128)(2,1)}, u32[]{:S(2)}, u32[]{:S(2)}) async-start(bf16[16,1,12,2048]{3,2,1,0:T(8,128)(2,1)} %bitcast.2), calls=%async_computation | async-start | bytes 2097152 | tf_op jit(solution)/shard_map/all_to_all | solution.py:45
  31.8 0.0 copy-done.1
  31.8 0.0 copy-done.6
  31.8 0.4 convolution_convert_fusion
  32.3 1.2 reshape.88
  33.4 43.3 %all-to-all-done = bf16[16,1,12,2048]{3,2,1,0:T(8,128)(2,1)} async-done(((bf16[16,1,12,2048]{3,2,1,0:T(8,128)(2,1)}), bf16[16,1,12,2048]{3,2,1,0:T(8,128)(2,1)}, u32[]{:S(2)}, u32[]{:S(2)}) %all-to-all-start) | async-done | bytes 786464 | tf_op jit(solution)/shard_map/all_to_all | solution.py:45
  76.7 13.2 %all-to-all-start.2 = ((bf16[16,1,12,2048]{3,2,1,0:T(8,128)(2,1)}), bf16[16,1,12,2048]{3,2,1,0:T(8,128)(2,1)S(1)}, u32[]{:S(2)}, u32[]{:S(2)}) async-start(bf16[16,1,12,2048]{3,2,1,0:T(8,128)(2,1)} %bitcast.22), calls=%async_computation.2 | async-start | bytes 2097152 | tf_op jit(solution)/shard_map/all_to_all | solution.py:46
  89.9 0.0 copy-done
  89.9 0.0 copy-start.3
  89.9 2.0 fusion.13
  92.0 0.0 copy-done.3
  92.0 1.9 fusion.16
  93.9 41.2 %all-to-all-done.2 = bf16[16,1,12,2048]{3,2,1,0:T(8,128)(2,1)S(1)} async-done(((bf16[16,1,12,2048]{3,2,1,0:T(8,128)(2,1)}), bf16[16,1,12,2048]{3,2,1,0:T(8,128)(2,1)S(1)}, u32[]{:S(2)}, u32[]{:S(2)}) %all-to-all-start.2) | async-done | bytes 786464 | tf_op jit(solution)/shard_map/all_to_all | solution.py:46
  135.2 2.5 fusion.19
  137.7 0.0 copy-start.4
  137.7 0.7 fusion.9
  138.4 0.0 copy-done.5
  138.4 0.7 copy-done.4
  139.1 0.7 fusion.2
  139.8 1.5 copy.24
  141.3 12.8 %all-to-all-start.3 = ((bf16[16,1,12,2048]{3,2,1,0:T(8,128)(2,1)}), bf16[16,1,12,2048]{3,2,1,0:T(8,128)(2,1)S(1)}, u32[]{:S(2)}, u32[]{:S(2)}) async-start(bf16[16,1,12,2048]{3,2,1,0:T(8,128)(2,1)} %copy.24), calls=%async_computation.3 | async-start | bytes 2097152 | tf_op jit(solution)/shard_map/all_to_all | solution.py:74
  154.1 0.1 fusion.35
  154.2 2.0 fusion.1
  156.2 1.4 copy.21
  157.7 41.7 %all-to-all-done.3 = bf16[16,1,12,2048]{3,2,1,0:T(8,128)(2,1)S(1)} async-done(((bf16[16,1,12,2048]{3,2,1,0:T(8,128)(2,1)}), bf16[16,1,12,2048]{3,2,1,0:T(8,128)(2,1)S(1)}, u32[]{:S(2)}, u32[]{:S(2)}) %all-to-all-start.3) | async-done | bytes 786464 | tf_op jit(solution)/shard_map/all_to_all | solution.py:74
  199.4 12.9 %all-to-all-start.1 = ((bf16[16,1,12,2048]{3,2,1,0:T(8,128)(2,1)}), bf16[16,1,12,2048]{3,2,1,0:T(8,128)(2,1)}, u32[]{:S(2)}, u32[]{:S(2)}) async-start(bf16[16,1,12,2048]{3,2,1,0:T(8,128)(2,1)} %copy.21), calls=%async_computation.1 | async-start | bytes 2097152 | tf_op jit(solution)/shard_map/all_to_all | solution.py:73
  212.2 0.2 all-reduce.3.cloned.1.call-start
  212.5 2.0 convolution_bitcast_fusion
  214.5 4.9 %copy.25 = f32[1,384,2048]{2,0,1:T(1,128)} copy(f32[1,384,2048]{2,1,0:T(8,128)S(1)} %convolution_bitcast_fusion) | data formatting | bytes 6291456 | tf_op jit(solution)/shard_map/secf,secd->efd/dot_general | solution.py:8
  219.4 0.0 all-reduce.3.cloned.1.call-update
  219.4 1.3 dynamic-slice
  221.3 223.6 %all-reduce.3.cloned.1.call-done = f32[1,384,2048]{2,0,1:T(1,128)} async-done(((f32[1,384,2048]{2,0,1:T(1,128)}), f32[1,384,2048]{2,0,1:T(1,128)}) %all-reduce.3.cloned.1.call-update) | async-done | bytes 3145744
  445.0 1.4 constant_dynamic-slice_fusion
  446.4 0.2 reshape.92
  446.6 1.1 convolution_convert_fusion.3
  447.7 0.0 all-to-all-done.1
  447.7 1.4 reshape.87
  449.1 0.0 copy-done.2
  449.1 1.8 fusion.23
  (2 shorter events, 0.0 us)
Async XLA Ops:
  7.2 82.8 %copy-start = (bf16[1,2048,384]{2,1,0:T(8,128)(2,1)S(1)}, bf16[1,2048,384]{2,1,0:T(8,128)(2,1)}, u32[]{:S(2)}) copy-start(bf16[1,2048,384]{2,1,0:T(8,128)(2,1)} %param.11) | copy-start | bytes 4718596
  11.1 20.7 %copy-start.1 = (bf16[128,2048]{1,0:T(8,128)(2,1)S(1)}, bf16[128,2048]{1,0:T(8,128)(2,1)}, u32[]{:S(2)}) copy-start(bf16[128,2048]{1,0:T(8,128)(2,1)} %param.10) | copy-start | bytes 1572868
  11.1 20.7 %copy-start.6 = (f32[128,1]{0,1:T(1,128)S(1)}, f32[128,1]{0,1:T(1,128)}, u32[]{:S(2)}) copy-start(f32[128,1]{0,1:T(1,128)} %param.9) | copy-start | bytes 1540
  12.3 64.4 %all-to-all-start = ((bf16[16,1,12,2048]{3,2,1,0:T(8,128)(2,1)}), bf16[16,1,12,2048]{3,2,1,0:T(8,128)(2,1)}, u32[]{:S(2)}, u32[]{:S(2)}) async-start(bf16[16,1,12,2048]{3,2,1,0:T(8,128)(2,1)} %bitcast.2), calls=%async_computation | async-start | bytes 2097152 | tf_op jit(solution)/shard_map/all_to_all | solution.py:45
  76.7 58.4 %all-to-all-start.2 = ((bf16[16,1,12,2048]{3,2,1,0:T(8,128)(2,1)}), bf16[16,1,12,2048]{3,2,1,0:T(8,128)(2,1)S(1)}, u32[]{:S(2)}, u32[]{:S(2)}) async-start(bf16[16,1,12,2048]{3,2,1,0:T(8,128)(2,1)} %bitcast.22), calls=%async_computation.2 | async-start | bytes 2097152 | tf_op jit(solution)/shard_map/all_to_all | solution.py:46
  89.9 2.1 copy-start.3
  135.2 3.3 copy-start.5
  137.7 1.4 copy-start.4
  141.3 58.0 %all-to-all-start.3 = ((bf16[16,1,12,2048]{3,2,1,0:T(8,128)(2,1)}), bf16[16,1,12,2048]{3,2,1,0:T(8,128)(2,1)S(1)}, u32[]{:S(2)}, u32[]{:S(2)}) async-start(bf16[16,1,12,2048]{3,2,1,0:T(8,128)(2,1)} %copy.24), calls=%async_computation.3 | async-start | bytes 2097152 | tf_op jit(solution)/shard_map/all_to_all | solution.py:74
  199.4 248.4 %all-to-all-start.1 = ((bf16[16,1,12,2048]{3,2,1,0:T(8,128)(2,1)}), bf16[16,1,12,2048]{3,2,1,0:T(8,128)(2,1)}, u32[]{:S(2)}, u32[]{:S(2)}) async-start(bf16[16,1,12,2048]{3,2,1,0:T(8,128)(2,1)} %copy.21), calls=%async_computation.1 | async-start | bytes 2097152 | tf_op jit(solution)/shard_map/all_to_all | solution.py:73
  212.2 232.8 %all-reduce.3.cloned.1.call-start = ((), (), s32[]{:S(2)}) async-start(), calls=%async_computation.4 | async-start | bytes 6291456
  447.7 1.4 copy-start.2
Sparse Core Ops, SparseCore 0:
  219.5 225.3 all-reduce.2
where the time goes:
time: 460 us; the launch traced here: 458 us
  waiting for transfers between devices  350 us (76%)
  starting transfers between devices  58.5 us (13%)
  matrix products  16.7 us (4%)
  local copies, waits for them, and re-layouts  15.2 us (3%)
  between operations  14.9 us (3%)
    unnamed x2, waiting for transfers between devices  224 us
    all_to_all x1, waiting for transfers between devices, shards(): lax.all_to_all(send_rows, 'ep', split_axis=0, concat_axis=0, tiled=True)  43.3 us
    all_to_all x1, waiting for transfers between devices, shards(): lax.all_to_all(input_back, 'ep', split_axis=0, concat_axis=0, tiled=True)  41.7 us
    all_to_all x1, waiting for transfers between devices, shards(): lax.all_to_all(send_grad, 'ep', split_axis=0, concat_axis=0, tiled=True)  41.2 us
    all_to_all x1, starting transfers between devices, shards(): lax.all_to_all(send_rows, 'ep', split_axis=0, concat_axis=0, tiled=True)  19.5 us
    all_to_all x1, starting transfers between devices, shards(): lax.all_to_all(send_grad, 'ep', split_axis=0, concat_axis=0, tiled=True)  13.2 us
    all_to_all x1, starting transfers between devices, shards(): lax.all_to_all(expert_out, 'ep', split_axis=0, concat_axis=0, tiled=True)  12.9 us
    all_to_all x1, starting transfers between devices, shards(): lax.all_to_all(input_back, 'ep', split_axis=0, concat_axis=0, tiled=True)  12.8 us
  transfers between devices with their start and end apart: 5, of which 4 were waited for; matrix products, arithmetic and copies ran while one was open for 4% of the time, Pallas kernels for 0%

commit v1 on v0

v1 whole, which is shorter than its diff:
```python
import jax
import jax.numpy as jnp
import numpy as np
from jax import lax
from jax.experimental import pallas as pl
from jax.experimental.pallas import tpu as pltpu
from jax.sharding import PartitionSpec as P

NX, NY, NZ = 4, 8, 16
TOK, WIDTH, FFW = 128, 2048, 384
CAP = 12
HALF = WIDTH // 2
BLK = 4 * CAP
ROWS = NZ * BLK
SLOTS = NZ * CAP
GROWS = WIDTH // (NX * NY)
DROWS = FFW // NY
QCOL = WIDTH // NX
MESH = pl.DeviceIdType.MESH
F32 = jnp.float32
BF16 = jnp.bfloat16
NT = (((1,), (1,)), ((), ()))


def dot(a, b):
    return jnp.dot(a, b, preferred_element_type=F32)


def dot_nt(a, b):
    return lax.dot_general(a, b, NT, preferred_element_type=F32)


def kernel(
    x_hbm, cot_hbm, ids_row, ids_col, gw_ref, wg_hbm, wu_hbm, wd_hbm, perm_hbm, wantc,
    out_ref, tgrad_ref, ggrad_ref, dgrad_ref,
    x, cot, z, wg, wu, wd, perm, send, recv, xall, yall, rsend, rrecv,
    dw, dwb, xrecv, ysend, yb, yrecv, zsend, zrecv, fsend, frecv,
    loc_sem, s1, r1, s2, r2, wzs, wzr, wxs, wxr, wys, wyr,
    dxs, dxr, dys, dyr, dzs, dzr, fs, fr,
):
    rep = lax.axis_index("rep")
    pz = lax.axis_index("ep")
    core = lax.rem(rep, 2)
    px = lax.rem(rep // 2, NX)
    py = rep // (2 * NX)
    other = 1 - core

    def dev(y, x_, c, z_):
        return ((y * NX + x_) * 2 + c, z_)

    def mod(v, n):
        return lax.rem(v + n, n)

    def at_z(off, c):
        return dev(py, px, c, mod(pz + off, NZ))

    tie = 4 - 8 * core

    def remote(src, dst, ss, rs, target):
        return pltpu.make_async_remote_copy(
            src_ref=src, dst_ref=dst, send_sem=ss, recv_sem=rs,
            device_id=target, device_id_type=MESH,
        )

    barrier = pltpu.get_barrier_semaphore()
    peers = [at_z(o, core) for o in (-4, -3, -2, -1, 1, 2, 3, 4, 8)]
    peers += [at_z(o, other) for o in (-3, -2, -1, 0, 1, 2, 3, 8)] + [at_z(tie, other)]
    for k in range(1, NX):
        peers.append(dev(py, mod(px + k, NX), core, pz))
        peers.append(dev(py, mod(px + k, NX), other, pz))
    for k in range(1, NY):
        peers.append(dev(mod(py + k, NY), px, core, pz))
    for peer in peers:
        pl.semaphore_signal(barrier, inc=1, device_id=peer, device_id_type=MESH)

    loads = [
        pltpu.make_async_copy(x_hbm, x, loc_sem.at[0]),
        pltpu.make_async_copy(cot_hbm, cot, loc_sem.at[1]),
        pltpu.make_async_copy(perm_hbm, perm, loc_sem.at[2]),
    ]
    for c in loads:
        c.start()
    wloads = [
        pltpu.make_async_copy(wg_hbm, wg, loc_sem.at[3]),
        pltpu.make_async_copy(wu_hbm, wu, loc_sem.at[4]),
        pltpu.make_async_copy(wd_hbm, wd, loc_sem.at[5]),
    ]

    @pl.when(core == 0)
    def _():
        for c in wloads:
            c.start()

    relr = lax.rem(ids_row[...] - pz + NZ, NZ)
    oh_r = (lax.broadcasted_iota(jnp.int32, (NZ, TOK), 0) == relr).astype(F32)
    up_tri = (
        lax.broadcasted_iota(jnp.int32, (TOK, TOK), 0)
        < lax.broadcasted_iota(jnp.int32, (TOK, TOK), 1)
    ).astype(F32)
    before = dot(oh_r.astype(BF16), up_tri.astype(BF16))
    slot_r = jnp.sum(before * oh_r, axis=0, keepdims=True).astype(jnp.int32)
    tgt_r = relr * CAP + slot_r

    ex = lax.broadcasted_iota(jnp.int32, (NZ, BLK, TOK), 0)
    row = lax.broadcasted_iota(jnp.int32, (NZ, BLK, TOK), 1)
    half = jnp.where(row >= 2 * CAP, 1, 0)
    row = row - 2 * CAP * half
    kind = jnp.where(row >= CAP, 1, 0)
    want = ex * CAP + row - CAP * kind
    quarter = jnp.where(want == tgt_r.reshape(1, 1, TOK), kind * 2 + half, -1)
    place = jnp.concatenate(
        [
            jnp.where(quarter == b, 1.0, 0.0).reshape(ROWS, TOK).astype(BF16)
            for b in range(4)
        ],
        axis=1,
    )
    for c in loads:
        c.wait()
    z[0:TOK, :] = x[:, :HALF]
    z[TOK : 2 * TOK, :] = x[:, HALF:]
    dout = (gw_ref[...] * cot[...].astype(F32)).astype(BF16)
    z[2 * TOK : 3 * TOK, :] = dout[:, :HALF]
    z[3 * TOK :, :] = dout[:, HALF:]

    @pl.loop(0, 4)
    def _(n):
        cols = pl.ds(pl.multiple_of(n * 256, 256), 256)
        send[:, :, cols] = dot(place, z[:, cols]).astype(BF16).reshape(NZ, BLK, 256)

    pl.semaphore_wait(barrier, len(peers))

    row_g = pl.multiple_of(py * (NX * GROWS) + px * GROWS, GROWS)
    row_d = pl.multiple_of(py * DROWS, 16)
    col_d = pl.multiple_of(px * QCOL, QCOL)

    def slices(y, x_, whole):
        if whole:
            g = pl.ds(pl.multiple_of(y * (NX * GROWS), NX * GROWS), NX * GROWS)
            return [(g, slice(None)), (g, slice(None)),
                    (pl.ds(pl.multiple_of(y * DROWS, 16), DROWS), slice(None))]
        g = pl.ds(pl.multiple_of(y * (NX * GROWS) + x_ * GROWS, GROWS), GROWS)
        d = (pl.ds(pl.multiple_of(y * DROWS, 16), DROWS),
             pl.ds(pl.multiple_of(x_ * QCOL, QCOL), QCOL))
        return [(g, slice(None)), (g, slice(None)), d]

    weights = (wg, wu, wd)
    own = slices(py, px, False)
    wz = [
        remote(h.at[i], w.at[i], wzs.at[m], wzr.at[m], at_z(8, core))
        for m, (h, w, i) in enumerate(zip((wg_hbm, wu_hbm, wd_hbm), weights, own))
    ]

    @pl.when(core == 1)
    def _():
        for c in wz:
            c.start()

    def out_copy(off, dc):
        d = mod(off + 8 * dc, NZ)
        k = core * 8 + off + 3 + core
        return remote(send.at[d], recv.at[k], s1.at[d], r1.at[k], at_z(off, dc))

    def back_copy(off, cs):
        k = cs * 8 + off + 3 + cs
        d = mod(off + 8 * core, NZ)
        return remote(rsend.at[k], rrecv.at[d], s2.at[k], r2.at[d], at_z(-off, cs))

    order = [(tie, core), (tie, other)]
    for o in (3, 2, 1):
        order += [(o, core), (-o, core), (o, other), (-o, other)]
    order += [(0, other)]
    outs = [out_copy(off, dc) for off, dc in order]
    for c in outs:
        c.start()
    mine_d = 8 * core
    mine_k = core * 8 + 3 + core
    self_out = pltpu.make_async_copy(send.at[mine_d], recv.at[mine_k], loc_sem.at[6])
    self_out.start()

    @pl.when(core == 1)
    def _():
        for c in wz:
            c.wait_recv()
        xs = []
        for k in (2, 1, 3):
            to = dev(py, mod(px + k, NX), core, pz)
            for m in range(3):
                xs.append(
                    remote(weights[m].at[own[m]], weights[m].at[own[m]],
                           wxs.at[k - 1, m], wxr.at[k - 1, m], to)
                )
        for c in xs:
            c.start()
        for k in (1, 3, 2):
            src = slices(py, mod(px - k, NX), False)
            for m in range(3):
                w = weights[m].at[src[m]]
                remote(w, w, wxs.at[k - 1, m], wxr.at[k - 1, m],
                       dev(py, mod(px + k, NX), core, pz)).wait_recv()
        ys = []
        depth = ((4, 3), (3, 4), (4, 3))
        for step in range(5):
            for m in range(3):
                for side, sign in ((0, 1), (1, -1)):
                    if step > depth[m][side]:
                        continue
                    w = weights[m].at[slices(mod(py - sign * step, NY), px, True)[m]]
                    to = dev(mod(py + sign, NY), px, core, pz)
                    if step > 0:
                        remote(w, w, wys.at[side, m, step - 1], wyr.at[side, m, step - 1],
                               to).wait_recv()
                    if step < depth[m][side]:
                        c = remote(w, w, wys.at[side, m, step], wyr.at[side, m, step], to)
                        c.start()
                        ys.append(c)
        for c in wz + xs + ys:
            c.wait_send()

    @pl.when(core == 0)
    def _():
        for c in wloads:
            c.wait()

    self_out.wait()

    def in_copy(off, cs):
        k = cs * 8 + off + 3 + cs
        d = mod(off + 8 * core, NZ)
        return remote(send.at[d], recv.at[k], s1.at[d], r1.at[k], at_z(-off, cs))

    sources = [(tie, core), (4 - 8 * other, other)]
    for o in (3, 2, 1):
        sources += [(o, core), (-o, core), (o, other), (-o, other)]
    sources += [(0, other)]
    for off, cs in sources:
        in_copy(off, cs).wait_recv()

    @pl.loop(0, 4)
    def _(n):
        cols = pl.ds(pl.multiple_of(n * 256, 256), 256)
        xall[:, cols] = dot(perm[0], recv[:, :, cols].reshape(ROWS, 256)).astype(BF16)

    xl, xr = xall[0:SLOTS, :], xall[SLOTS : 2 * SLOTS, :]
    dl, dr = xall[2 * SLOTS : 3 * SLOTS, :], xall[3 * SLOTS :, :]
    a = dot(xl, wg[:HALF, :]) + dot(xr, wg[HALF:, :])
    b = dot(xl, wu[:HALF, :]) + dot(xr, wu[HALF:, :])
    dh = dot_nt(dl, wd[:, :HALF]) + dot_nt(dr, wd[:, HALF:])
    s = 1.0 / (1.0 + jnp.exp(-a))
    act = a * s
    hf = act * b
    h = hf.astype(BF16)
    da = (dh * b * s * (1.0 + a * (1.0 - s))).astype(BF16)
    db = (dh * act).astype(BF16)
    ht = jnp.transpose(hf).astype(BF16)
    for j in range(NX):
        d0 = 2 * SLOTS + SLOTS * (j // 2)
        c0 = QCOL * (j % 2)
        piece = dot(ht, xall[d0 : d0 + SLOTS, c0 : c0 + QCOL])
        dw[j] = piece
        dwb[j] = piece.astype(BF16)
    dx_copies = []
    for k in (2, 1, 3):
        to = mod(px + k, NX)
        c = remote(dwb.at[to], xrecv.at[k - 1], dxs.at[k - 1], dxr.at[k - 1],
                   dev(py, to, core, pz))
        c.start()
        dx_copies.append(c)

    for n in range(4):
        q, c0 = n // 2, QCOL * (n % 2)
        cols = slice(n * QCOL, (n + 1) * QCOL)
        yall[q * SLOTS : (q + 1) * SLOTS, c0 : c0 + QCOL] = dot(h, wd[:, cols]).astype(BF16)
        back = dot_nt(da, wg[cols, :]) + dot_nt(db, wu[cols, :])
        yall[(2 + q) * SLOTS : (3 + q) * SLOTS, c0 : c0 + QCOL] = back.astype(BF16)

    @pl.loop(0, 4)
    def _(n):
        cols = pl.ds(pl.multiple_of(n * 256, 256), 256)
        rsend[:, :, cols] = dot(perm[1], yall[:, cols]).astype(BF16).reshape(NZ, BLK, 256)

    backs = [back_copy(off, cs) for off, cs in sources]
    for c in backs:
        c.start()
    self_back = pltpu.make_async_copy(rsend.at[mine_k], rrecv.at[mine_d], loc_sem.at[7])
    self_back.start()

    for c in dx_copies:
        c.wait_recv()
    for i in range(NY):
        rr = slice(i * DROWS, (i + 1) * DROWS)
        part = dw[px, rr, :]
        for k in range(NX - 1):
            part = part + xrecv[k, rr, :].astype(F32)
        ysend[i] = part
        yb[i] = part.astype(BF16)
    dy_copies = []
    for k in (4, 3, 5, 2, 6, 1, 7):
        to = mod(py + k, NY)
        c = remote(yb.at[to], yrecv.at[k - 1], dys.at[k - 1], dyr.at[k - 1],
                   dev(to, px, core, pz))
        c.start()
        dy_copies.append(c)
    for c in dy_copies:
        c.wait_recv()
    part = ysend[py]
    for k in range(NY - 1):
        part = part + yrecv[k].astype(F32)
    zsend[...] = part
    dz = remote(zsend, zrecv, dzs.at[0], dzr.at[0], at_z(8, other))

    @pl.when(core == 1)
    def _():
        dz.start()

    @pl.when(core == 0)
    def _():
        dz.wait_recv()
        total = zsend[...] + zrecv[...]
        for i in range(2 * NX):
            fsend[i, 0:6, :] = total[i * 6 : (i + 1) * 6, :]
            fsend[i, 6:8, :] = jnp.zeros((2, QCOL), F32)
        mine = pltpu.make_async_copy(fsend.at[2 * px], frecv.at[px], loc_sem.at[8])
        mine.start()
        fins = [remote(fsend.at[2 * px + 1], frecv.at[px], fs.at[0, 1], fr.at[px],
                       dev(py, px, 1, pz))]
        for k in range(1, NX):
            to = mod(px + k, NX)
            for c in range(2):
                fins.append(
                    remote(fsend.at[2 * to + c], frecv.at[px], fs.at[k, c], fr.at[px],
                           dev(py, to, c, pz))
                )
        for c in fins:
            c.start()
        mine.wait()
        for k in range(1, NX):
            src = mod(px + k, NX)
            remote(fsend.at[0], frecv.at[src], fs.at[k, 0], fr.at[src],
                   dev(py, src, 0, pz)).wait_recv()
        for c in fins:
            c.wait_send()

    @pl.when(core == 1)
    def _():
        for src in range(NX):
            remote(fsend.at[0], frecv.at[src], fs.at[0, 0], fr.at[src],
                   dev(py, src, 0, pz)).wait_recv()
        dz.wait_send()

    for j in range(NX):
        dgrad_ref[0, :, j * QCOL : (j + 1) * QCOL] = frecv[j, 0:6, :]

    relc = lax.rem(ids_col[...] - pz + NZ, NZ)
    oh_c = (lax.broadcasted_iota(jnp.int32, (TOK, TOK), 1) == relc).astype(F32)
    lo_tri = (
        lax.broadcasted_iota(jnp.int32, (TOK, TOK), 0)
        > lax.broadcasted_iota(jnp.int32, (TOK, TOK), 1)
    ).astype(F32)
    before_c = dot(lo_tri.astype(BF16), oh_c.astype(BF16))
    slot_c = jnp.sum(before_c * oh_c, axis=1, keepdims=True).astype(jnp.int32)
    tgt_c = relc * CAP + slot_c
    takes = [
        jnp.where(wantc[b : b + 1, :] == tgt_c, 1.0, 0.0).astype(BF16) for b in range(4)
    ]
    self_back.wait()

    def ret_copy(off, dc):
        d = mod(off + 8 * dc, NZ)
        k = core * 8 + off + 3 + core
        return remote(rsend.at[k], rrecv.at[d], s2.at[k], r2.at[d], at_z(off, dc))

    for off, dc in order:
        ret_copy(off, dc).wait_recv()
    gsum = jnp.zeros((TOK, 1), F32)
    for n in range(4):
        cols = slice(n * 256, (n + 1) * 256)
        src = rrecv[:, :, cols].reshape(ROWS, 256)
        for q in range(2):
            full = slice(q * HALF + n * 256, q * HALF + (n + 1) * 256)
            o = dot(takes[q], src)
            out_ref[:, full] = (gw_ref[...] * o).astype(BF16)
            gsum = gsum + jnp.sum(cot[:, full].astype(F32) * o, axis=1, keepdims=True)
            tgrad_ref[:, full] = dot(takes[2 + q], src).astype(BF16)
    ggrad_ref[...] = gsum

    for c in outs + backs + dx_copies + dy_copies:
        c.wait_send()


def tables():
    perm = np.zeros((ROWS, ROWS), np.float32)
    want = np.full((8, ROWS), -1, np.int32)
    for r in range(ROWS):
        k, w = divmod(r, BLK)
        half, w = divmod(w, 2 * CAP)
        kind, s = divmod(w, CAP)
        b = kind * 2 + half
        perm[b * SLOTS + k * CAP + s, r] = 1.0
        want[b, r] = k * CAP + s
    return np.stack([perm, perm.T]), want


def shards(tokens, expert_ids, gate_weights, cotangent, gate_weight, up_weight, down_weight):
    perm, want = tables()
    hbm = pl.BlockSpec(memory_space=pl.ANY)
    vmem = pl.BlockSpec(memory_space=pltpu.VMEM)
    dma = pltpu.SemaphoreType.DMA
    return pl.pallas_call(
        kernel,
        out_shape=(
            jax.ShapeDtypeStruct((TOK, WIDTH), BF16),
            jax.ShapeDtypeStruct((TOK, WIDTH), BF16),
            jax.ShapeDtypeStruct((TOK, 1), F32),
            jax.ShapeDtypeStruct((1, FFW // (2 * NX * NY), WIDTH), F32),
        ),
        in_specs=[hbm, hbm, vmem, vmem, vmem, hbm, hbm, hbm, hbm, vmem],
        out_specs=(vmem, vmem, vmem, vmem),
        scratch_shapes=[
            pltpu.VMEM((TOK, WIDTH), BF16),
            pltpu.VMEM((TOK, WIDTH), BF16),
            pltpu.VMEM((4 * TOK, HALF), BF16),
            pltpu.VMEM((WIDTH, FFW), BF16),
            pltpu.VMEM((WIDTH, FFW), BF16),
            pltpu.VMEM((FFW, WIDTH), BF16),
            pltpu.VMEM((2, ROWS, ROWS), BF16),
            pltpu.VMEM((NZ, BLK, HALF), BF16),
            pltpu.VMEM((NZ, BLK, HALF), BF16),
            pltpu.VMEM((ROWS, HALF), BF16),
            pltpu.VMEM((ROWS, HALF), BF16),
            pltpu.VMEM((NZ, BLK, HALF), BF16),
            pltpu.VMEM((NZ, BLK, HALF), BF16),
            pltpu.VMEM((NX, FFW, QCOL), F32),
            pltpu.VMEM((NX, FFW, QCOL), BF16),
            pltpu.VMEM((NX - 1, FFW, QCOL), BF16),
            pltpu.VMEM((NY, DROWS, QCOL), F32),
            pltpu.VMEM((NY, DROWS, QCOL), BF16),
            pltpu.VMEM((NY - 1, DROWS, QCOL), BF16),
            pltpu.VMEM((DROWS, QCOL), F32),
            pltpu.VMEM((DROWS, QCOL), F32),
            pltpu.VMEM((2 * NX, 8, QCOL), F32),
            pltpu.VMEM((NX, 8, QCOL), F32),
            dma((9,)),
            dma((NZ,)), dma((NZ,)), dma((NZ,)), dma((NZ,)),
            dma((3,)), dma((3,)), dma((3, 3)), dma((3, 3)),
            dma((2, 3, 4)), dma((2, 3, 4)),
            dma((NX - 1,)), dma((NX - 1,)), dma((NY - 1,)), dma((NY - 1,)),
            dma((1,)), dma((1,)), dma((NX, 2)), dma((NX,)),
        ],
        compiler_params=pltpu.CompilerParams(
            collective_id=0, has_side_effects=True, vmem_limit_bytes=56 * 1024 * 1024
        ),
        cost_estimate=pl.CostEstimate(
            flops=6_000_000_000, bytes_accessed=16_000_000, transcendentals=100_000
        ),
    )(
        tokens, cotangent, expert_ids.reshape(1, TOK), expert_ids, gate_weights,
        gate_weight[0], up_weight[0], down_weight[0],
        jnp.asarray(perm, BF16), jnp.asarray(want),
    )


def solution(mesh):
    rows = P(("rep", "ep"), None)
    weight = P("ep", None, None)
    return jax.shard_map(
        shards,
        mesh=mesh,
        in_specs=(rows, rows, rows, rows, weight, weight, weight),
        out_specs=(rows, rows, rows, P("ep", "rep", None)),
        check_vma=False,
    )
```

time: 460 us -> 134 us (0.29)
  waiting for transfers between devices: 350 us -> 0 us
  Pallas kernels: 0 us -> 125 us
  starting transfers between devices: 58.5 us -> 0 us
  matrix products: 16.7 us -> 0 us
  between operations: 14.9 us -> 0.65 us
  local copies, waits for them, and re-layouts: 15.2 us -> 8.45 us
    unnamed x2 -> x0, waiting for transfers between devices: 224 us -> none
    all_to_all x4 -> x0, waiting for transfers between devices: 126 us -> none  [the longest x1 43.3 us: shards(): lax.all_to_all(send_rows, 'ep', split_axis=0, concat_axis=0, tiled=True)]
    pallas_call x0 -> x1, Pallas kernels: none -> 125 us  [shards(): pl.pallas_call(kernel, out_shape=(jax.ShapeDtypeStruct((TOK, WIDTH), BF16...]
    all_to_all x4 -> x0, starting transfers between devices: 58.3 us -> none  [the longest x1 19.5 us: shards(): lax.all_to_all(send_rows, 'ep', split_axis=0, concat_axis=0, tiled=True)]
    dot_general x11 -> x0, matrix products: 16.7 us -> none  [the longest x1 2.53 us: shards(): jnp.einsum('secd,efd->secf', recv_grad, down_weight, preferred_element_ty...]
    dot_general x1 -> x0, local copies, waits for them, and re-layouts: 4.91 us -> none  [group_grad(): jnp.einsum('secf,secd->efd', hidden, recv_grad, preferred_element_type=jn...]
  transfers between devices with their start and end apart: 5 -> 0, of which waited for: 4 -> 0; matrix products, arithmetic and copies ran while one was open for 4% -> 0% of each run, Pallas kernels for 0% -> 0%
where the time goes in v1:
time: 134 us
  Pallas kernels  125 us (93%)
  local copies, waits for them, and re-layouts  8.45 us (6%)
    pallas_call x1, Pallas kernels, shards(): pl.pallas_call(kernel, out_shape=(jax.ShapeDtypeStruct((TOK, WIDTH), BF16...  125 us
    unnamed x6, local copies, waits for them, and re-layouts  5.46 us
    pallas_call x2, local copies, waits for them, and re-layouts, shards(): pl.pallas_call(kernel, out_shape=(jax.ShapeDtypeStruct((TOK, WIDTH), BF16...  2.99 us

profile of v1, /device:TPU:1, one launch (start us, length us, event | category | flops | bytes accessed | tf_op | source)
XLA Modules:
  0.0 134.0 jit_solution(2332221493914238487)
XLA Ops:
  0.6 1.4 %copy.14.gw_ref = f32[128,1]{1,0:T(8,128)} copy(f32[128,1]{0,1:T(1,128)} %param.11) | data formatting | bytes 1024 | tf_op args[2]
  2.0 1.4 %copy.13.ids_col = s32[128,1]{1,0:T(8,128)} copy(s32[128,1]{0,1:T(1,128)} %param.10) | data formatting | bytes 1024 | tf_op args[1]
  3.4 124.9 %shard_map.120 = (bf16[128,2048]{1,0:T(8,128)(2,1)}, bf16[128,2048]{1,0:T(8,128)(2,1)}, f32[128,1]{1,0:T(8,128)}, f32[1,6,2048]{2,1,0:T(8,128)}) custom-call(bf16[128,2048]{1,0:T(8,128)(2,1)} %x_hbm.1, bf16[128,2048]{1,0:T(8,128)(2,1)} %cot_hbm.1, s32[1,128]{1,0:T(1,128)} %bitcast.4, s32[128,1]{1,0:T(8,128)} %copy.13.ids_col, f32[128,1]{1,0:T(8,128)} %copy.14.gw_ref, ...), custom_call_target="tpu_custom_call" | custom-call | flops 6000000000 | bytes 16000000 | tf_op jit(solution)/shard_map/pallas_call | solution.py:409
  128.3 0.0 copy-start
  128.3 1.5 %copy.15 = f32[128,1]{0,1:T(1,128)} copy(f32[128,1]{1,0:T(8,128)} %get-tuple-element.6) | data formatting | bytes 1024 | tf_op jit(solution)/shard_map/pallas_call | solution.py:409
  129.8 1.5 %copy.16 = f32[1,6,2048]{2,0,1:T(1,128)} copy(f32[1,6,2048]{2,1,0:T(8,128)} %get-tuple-element.7) | data formatting | bytes 98304 | tf_op jit(solution)/shard_map/pallas_call | solution.py:409
  131.3 1.9 %copy.19 = bf16[128,2048]{1,0:T(8,128)(2,1)} copy(bf16[128,2048]{1,0:T(8,128)(2,1)} %get-tuple-element.12) | data formatting | bytes 1048576
  133.2 0.0 copy-done
  133.2 0.8 copy.20
Async XLA Ops:
  128.3 4.9 %copy-start = (bf16[128,2048]{1,0:T(8,128)(2,1)S(1)}, bf16[128,2048]{1,0:T(8,128)(2,1)}, u32[]{:S(2)}) copy-start(bf16[128,2048]{1,0:T(8,128)(2,1)} %get-tuple-element.13) | copy-start | bytes 1572868

commit v2 on v1

v2 whole, which is shorter than its diff:
```python
import jax
import jax.numpy as jnp
import numpy as np
from jax import lax
from jax.experimental import pallas as pl
from jax.experimental.pallas import tpu as pltpu
from jax.sharding import PartitionSpec as P

NX, NY, NZ = 4, 8, 16
TOK, WIDTH, FFW = 128, 2048, 384
CAP = 12
HALF = WIDTH // 2
BLK = 4 * CAP
FAR = 6
NEAR = NZ - FAR
FROWS, NROWS = FAR * BLK, NEAR * BLK
FPAD, NPAD = 80, 128
GROWS = WIDTH // (NX * NY)
DROWS = FFW // NY
QCOL = WIDTH // NX
MID = FFW // 2
MESH = pl.DeviceIdType.MESH
F32 = jnp.float32
BF16 = jnp.bfloat16
NT = (((1,), (1,)), ((), ()))
ALL = slice(None)


def dot(a, b):
    return jnp.dot(a, b, preferred_element_type=F32)


def dot_nt(a, b):
    return lax.dot_general(a, b, NT, preferred_element_type=F32)


def ds(start, size):
    return pl.ds(pl.multiple_of(start, size), size)


def kernel(
    x_hbm, cot_hbm, ids_row, gw_row, wg_hbm, wu_hbm, wd_hbm, pf_hbm, pft_hbm, pn_hbm, pnt_hbm,
    wantc,
    out_ref, tgrad_ref, ggrad_ref, dgrad_ref,
    x, cot, z, wg, wu, wd, pf, pft, pn, pnt, send, recv, xf, yf, xn, yn, rsend, rrecv,
    oacc, dw, dwb, opp, pure, msend, mrecv, ysum, yb, yrecv, zsend, zrecv, fsend, frecv,
    loc_sem, s1, r1, s2, r2, wzs, wzr, gxs, gxr, gys, gyr, uys, uyr, uxs, uxr,
    dxs, dxr, dys, dyr, dzs, dzr, fs, fr,
):
    rep = lax.axis_index("rep")
    pz = lax.axis_index("ep")
    core = lax.rem(rep, 2)
    px = lax.rem(rep // 2, NX)
    py = rep // (2 * NX)
    other = 1 - core

    def dev(y, x_, c, z_):
        return ((y * NX + x_) * 2 + c, z_)

    def mod(v, n):
        return lax.rem(v + n, n)

    def at_x(k):
        return dev(py, mod(px + k, NX), core, pz)

    def at_y(k):
        return dev(mod(py + k, NY), px, core, pz)

    def at_z(off, c):
        return dev(py, px, c, mod(pz + off, NZ))

    def remote(src, dst, ss, rs, target):
        return pltpu.make_async_remote_copy(
            src_ref=src, dst_ref=dst, send_sem=ss, recv_sem=rs,
            device_id=target, device_id_type=MESH,
        )

    tie, tie_other = 4 - 8 * core, 4 - 8 * other
    barrier = pltpu.get_barrier_semaphore()
    peers = [at_z(o, core) for o in (-4, -3, -2, -1, 1, 2, 3, 4, 8)]
    peers += [at_z(o, other) for o in (-3, -2, -1, 0, 1, 2, 3, 8)] + [at_z(tie, other)]
    for k in range(1, NX):
        peers.append(at_x(k))
        peers.append(dev(py, mod(px + k, NX), other, pz))
    for k in range(1, NY):
        peers.append(at_y(k))
    for peer in peers:
        pl.semaphore_signal(barrier, inc=1, device_id=peer, device_id_type=MESH)

    loads = [
        pltpu.make_async_copy(s, d, loc_sem.at[i])
        for i, (s, d) in enumerate(
            ((x_hbm, x), (cot_hbm, cot), (pf_hbm, pf), (pft_hbm, pft), (pn_hbm, pn), (pnt_hbm, pnt))
        )
    ]
    for c in loads:
        c.start()
    weights = (wg, wu, wd)
    wloads = [
        pltpu.make_async_copy(s, d, loc_sem.at[6 + i])
        for i, (s, d) in enumerate(zip((wg_hbm, wu_hbm, wd_hbm), weights))
    ]

    @pl.when(core == 0)
    def _():
        for c in wloads:
            c.start()

    def place_of(ids):
        u = lax.rem(ids - pz + (2 * NZ - 3), NZ)
        u = u + jnp.where((u >= 3) & (u < 8), 3, 0) - jnp.where((u >= 8) & (u < 11), 5, 0)
        return u

    lane = lax.broadcasted_iota(jnp.int32, (TOK, TOK), 1)
    sub = lax.broadcasted_iota(jnp.int32, (TOK, TOK), 0)
    eye = lane == sub
    q_r = place_of(ids_row[...])
    q_c = jnp.sum(jnp.where(eye, q_r, 0), axis=1, keepdims=True)
    gw_c = jnp.sum(jnp.where(eye, gw_row[...], 0.0), axis=1, keepdims=True)
    oh_r = (lax.broadcasted_iota(jnp.int32, (NZ, TOK), 0) == q_r).astype(F32)
    before = dot(oh_r.astype(BF16), (sub < lane).astype(F32).astype(BF16))
    slot_r = jnp.sum(before * oh_r, axis=0, keepdims=True).astype(jnp.int32)
    tgt_r = q_r * CAP + slot_r
    tgt_c = jnp.sum(jnp.where(eye, tgt_r, 0), axis=1, keepdims=True)

    def placing(first, count):
        ex = lax.broadcasted_iota(jnp.int32, (count, BLK, TOK), 0) + first
        row = lax.broadcasted_iota(jnp.int32, (count, BLK, TOK), 1)
        half = jnp.where(row >= 2 * CAP, 1, 0)
        row = row - 2 * CAP * half
        kind = jnp.where(row >= CAP, 1, 0)
        want = ex * CAP + row - CAP * kind
        quarter = jnp.where(want == tgt_r.reshape(1, 1, TOK), kind * 2 + half, -1)
        return jnp.concatenate(
            [
                jnp.where(quarter == b, 1.0, 0.0).reshape(count * BLK, TOK).astype(BF16)
                for b in range(4)
            ],
            axis=1,
        )

    for c in loads:
        c.wait()
    z[0:TOK, :] = x[:, :HALF]
    z[TOK : 2 * TOK, :] = x[:, HALF:]
    dout = (gw_c * cot[...].astype(F32)).astype(BF16)
    z[2 * TOK : 3 * TOK, :] = dout[:, :HALF]
    z[3 * TOK :, :] = dout[:, HALF:]

    pl.semaphore_wait(barrier, len(peers))

    own = (
        (ds(py * (NX * GROWS) + px * GROWS, GROWS), ALL),
        (ds(px * (NY * GROWS) + py * GROWS, GROWS), ALL),
        (ds(py * DROWS, DROWS), ds(px * QCOL, QCOL)),
    )
    wz = [
        remote(h.at[i], w.at[i], wzs.at[m], wzr.at[m], at_z(8, core))
        for m, (h, w, i) in enumerate(zip((wg_hbm, wu_hbm, wd_hbm), weights, own))
    ]

    @pl.when(core == 1)
    def _():
        for m in (1, 2, 0):
            wz[m].start()

    def as_source():
        far = [(tie, core, 1, 4 + core), (tie, other, 4, 4 + core)]
        for c in (core, other):
            far += [(3, c, 3 * c, 2 + core), (-3, c, 5 - 3 * c, core)]
        near = []
        for o in (2, -2, 1, -1):
            for c in (core, other):
                near.append((o, c, 13 + o - 5 * c, 10 + 2 * o + core))
        near.append((0, other, 13 - 5 * other, 10 + core))
        return far, near

    def as_expert():
        far = [(tie, core, 1, 4 + core), (tie_other, other, 4, 4 + other)]
        for c in (core, other):
            far += [(3, c, 3 * core, 2 + c), (-3, c, 5 - 3 * core, c)]
        near = []
        for o in (2, -2, 1, -1):
            for c in (core, other):
                near.append((o, c, 13 + o - 5 * core, 10 + 2 * o + c))
        near.append((0, other, 13 - 5 * core, 10 + other))
        return far, near

    def there(off, c, q, k, target):
        return remote(send.at[q], recv.at[k], s1.at[q], r1.at[k], target)

    def back(off, c, q, k, target):
        return remote(rsend.at[k], rrecv.at[q], s2.at[k], r2.at[q], target)

    def towards(e):
        return at_z(e[0], e[1])

    def whence(e):
        return at_z(-e[0], e[1])

    mine_q, mine_k = 13 - 5 * core, 10 + core
    src_far, src_near = as_source()
    exp_far, exp_near = as_expert()

    outs = []
    for first, count, group in ((0, FAR, src_far), (FAR, NEAR, src_near)):
        place = placing(first, count)

        @pl.loop(0, 4)
        def _(n):
            cols = ds(n * 256, 256)
            send[first : first + count, :, cols] = (
                dot(place, z[:, cols]).astype(BF16).reshape(count, BLK, 256)
            )

        for e in group:
            c = there(*e, towards(e))
            c.start()
            outs.append(c)
    self_out = pltpu.make_async_copy(send.at[mine_q], recv.at[mine_k], loc_sem.at[9])
    self_out.start()

    @pl.when(core == 1)
    def _():
        started = list(wz)

        def go(c):
            c.start()
            started.append(c)

        def y_slice(m, y):
            if m == 0:
                return wg.at[ds(y * (NX * GROWS), NX * GROWS), ALL]
            if m == 1:
                return wu.at[ds(px * (NY * GROWS) + y * GROWS, GROWS), ALL]
            return wd.at[ds(y * DROWS, DROWS), ds(px * QCOL, QCOL)]

        depth = ((4, 3), (3, 4), (3, 4))

        def chain(m, step):
            ss, rs = (gys, gyr) if m == 0 else (uys.at[m - 1], uyr.at[m - 1])
            for side, sign in ((0, 1), (1, -1)):
                if step > depth[m][side]:
                    continue
                w = y_slice(m, mod(py - sign * step, NY))
                if step > 0:
                    remote(w, w, ss.at[side, step - 1], rs.at[side, step - 1],
                           at_y(sign)).wait_recv()
                if step < depth[m][side]:
                    go(remote(w, w, ss.at[side, step], rs.at[side, step], at_y(sign)))

        def x_block(m, xx, part=None):
            if m == 1:
                n = NY * GROWS
                if part is None:
                    return wu.at[ds(xx * n, n), ALL]
                return wu.at[ds(xx * n + part * (n // 2), n // 2), ALL]
            rows = ALL if part is None else slice(part * MID, (part + 1) * MID)
            return wd.at[rows, ds(xx * QCOL, QCOL)]

        for m in (1, 2):
            wz[m].wait_recv()
            chain(m, 0)
        wz[0].wait_recv()
        w = wg.at[own[0]]
        for k in (2, 1, 3):
            go(remote(w, w, gxs.at[k - 1], gxr.at[k - 1], at_x(k)))
        for m in (1, 2):
            chain(m, 1)
        for k in (1, 3, 2):
            w = wg.at[ds(py * (NX * GROWS) + mod(px - k, NX) * GROWS, GROWS), ALL]
            remote(w, w, gxs.at[k - 1], gxr.at[k - 1], at_x(k)).wait_recv()
        chain(0, 0)
        for step in (2, 3, 4):
            for m in (1, 2):
                chain(m, step)
        for m in (1, 2):
            w = x_block(m, px)
            for side, sign in ((0, 1), (1, -1)):
                go(remote(w, w, uxs.at[m - 1, side, 0], uxr.at[m - 1, side, 0], at_x(sign)))
        chain(0, 1)
        for m in (1, 2):
            for side, sign in ((0, 1), (1, -1)):
                w = x_block(m, mod(px - sign, NX))
                remote(w, w, uxs.at[m - 1, side, 0], uxr.at[m - 1, side, 0],
                       at_x(sign)).wait_recv()
                w = x_block(m, mod(px - sign, NX), side)
                go(remote(w, w, uxs.at[m - 1, side, 1], uxr.at[m - 1, side, 1], at_x(sign)))
        for step in (2, 3, 4):
            chain(0, step)
        for m in (1, 2):
            for side, sign in ((0, 1), (1, -1)):
                w = x_block(m, mod(px + 2, NX), side)
                remote(w, w, uxs.at[m - 1, side, 1], uxr.at[m - 1, side, 1],
                       at_x(sign)).wait_recv()
        for c in started:
            c.wait_send()

    @pl.when(core == 0)
    def _():
        for c in wloads:
            c.wait()

    def gather_rows(first, count, pad, perm, dst):
        @pl.loop(0, 4)
        def _(n):
            cols = ds(n * 256, 256)
            rows = recv[first : first + count, :, cols].reshape(count * BLK, 256)
            dst[:, cols] = dot(perm[...], rows).astype(BF16)

        xl, xr = dst[0:pad, :], dst[pad : 2 * pad, :]
        dl, dr = dst[2 * pad : 3 * pad, :], dst[3 * pad :, :]
        a = dot(xl, wg[:HALF, :]) + dot(xr, wg[HALF:, :])
        b = dot(xl, wu[:HALF, :]) + dot(xr, wu[HALF:, :])
        dh = dot_nt(dl, wd[:, :HALF]) + dot_nt(dr, wd[:, HALF:])
        s = 1.0 / (1.0 + jnp.exp(-a))
        act = a * s
        hf = act * b
        da = (dh * b * s * (1.0 + a * (1.0 - s))).astype(BF16)
        db = (dh * act).astype(BF16)
        return hf, da, db

    def results(first, count, pad, perm_t, src, hf, da, db):
        h = hf.astype(BF16)
        for n in range(4):
            q, c0 = n // 2, QCOL * (n % 2)
            cols = slice(n * QCOL, (n + 1) * QCOL)
            src[q * pad : (q + 1) * pad, c0 : c0 + QCOL] = dot(h, wd[:, cols]).astype(BF16)
            grad = dot_nt(da, wg[cols, :]) + dot_nt(db, wu[cols, :])
            src[(2 + q) * pad : (3 + q) * pad, c0 : c0 + QCOL] = grad.astype(BF16)

        @pl.loop(0, 4)
        def _(n):
            cols = ds(n * 256, 256)
            rsend[first : first + count, :, cols] = (
                dot(perm_t[...], src[:, cols]).astype(BF16).reshape(count, BLK, 256)
            )

    backs = []
    for e in exp_far:
        there(*e, whence(e)).wait_recv()
    hf_far, da, db = gather_rows(0, FAR, FPAD, pf, xf)
    results(0, FAR, FPAD, pft, yf, hf_far, da, db)
    for e in exp_far:
        c = back(*e, whence(e))
        c.start()
        backs.append(c)

    self_out.wait()
    for e in exp_near:
        there(*e, whence(e)).wait_recv()
    hf, da, db = gather_rows(FAR, NEAR, NPAD, pn, xn)

    htf = jnp.transpose(hf_far).astype(BF16)
    htn = jnp.transpose(hf).astype(BF16)
    for j in range(NX):
        q, c0 = 2 + j // 2, QCOL * (j % 2)
        piece = dot(htf, xf[q * FPAD : (q + 1) * FPAD, c0 : c0 + QCOL])
        piece = piece + dot(htn, xn[q * NPAD : (q + 1) * NPAD, c0 : c0 + QCOL])
        dw[j] = piece
        dwb[j] = piece.astype(BF16)
    right, left, across = mod(px + 1, NX), mod(px - 1, NX), mod(px + 2, NX)
    lo, hi = slice(0, MID), slice(MID, FFW)
    dx_copies = [
        remote(dwb.at[across, lo], opp.at[0], dxs.at[0], dxr.at[0], at_x(1)),
        remote(dwb.at[across, hi], opp.at[1], dxs.at[1], dxr.at[1], at_x(-1)),
        remote(dwb.at[right, hi], pure.at[0], dxs.at[2], dxr.at[2], at_x(1)),
        remote(dwb.at[left, lo], pure.at[1], dxs.at[3], dxr.at[3], at_x(-1)),
    ]
    for c in dx_copies:
        c.start()

    results(FAR, NEAR, NPAD, pnt, yn, hf, da, db)
    for e in exp_near:
        c = back(*e, whence(e))
        c.start()
        backs.append(c)
    self_back = pltpu.make_async_copy(rsend.at[mine_k], rrecv.at[mine_q], loc_sem.at[10])
    self_back.start()

    merged = [
        remote(msend.at[0], mrecv.at[0], dxs.at[4], dxr.at[4], at_x(1)),
        remote(msend.at[1], mrecv.at[1], dxs.at[5], dxr.at[5], at_x(-1)),
    ]
    dx_copies[0].wait_recv()
    msend[0] = (dw[right, lo, :] + opp[0].astype(F32)).astype(BF16)
    merged[0].start()
    dx_copies[1].wait_recv()
    msend[1] = (dw[left, hi, :] + opp[1].astype(F32)).astype(BF16)
    merged[1].start()
    for c in dx_copies[2:] + merged:
        c.wait_recv()
    for i in range(NY):
        top = i < NY // 2
        rr = slice(i * DROWS, (i + 1) * DROWS)
        r0 = i * DROWS - (0 if top else MID)
        rm = slice(r0, r0 + DROWS)
        m, p = (0, 1) if top else (1, 0)
        part = dw[px, rr, :] + mrecv[m, rm, :].astype(F32) + pure[p, rm, :].astype(F32)
        ysum[i] = part
        yb[i] = part.astype(BF16)
    dy_copies = []
    for k in (4, 3, 5, 2, 6, 1, 7):
        c = remote(yb.at[mod(py + k, NY)], yrecv.at[k - 1], dys.at[k - 1], dyr.at[k - 1], at_y(k))
        c.start()
        dy_copies.append(c)
    for c in dy_copies:
        c.wait_recv()
    part = ysum[py]
    for k in range(NY - 1):
        part = part + yrecv[k].astype(F32)
    zsend[...] = part.astype(BF16)
    dz = remote(zsend, zrecv, dzs.at[0], dzr.at[0], at_z(8, other))

    @pl.when(core == 1)
    def _():
        dz.start()

    def taking(b, first, count):
        rows = slice(first * BLK, (first + count) * BLK)
        return jnp.where(wantc[b : b + 1, rows] == tgt_c, 1.0, 0.0).astype(BF16)

    takes = [taking(b, 0, FAR) for b in range(4)]
    for e in src_far:
        back(*e, towards(e)).wait_recv()
    for n in range(4):
        cols = slice(n * 256, (n + 1) * 256)
        src = rrecv[0:FAR, :, cols].reshape(FROWS, 256)
        for b in range(4):
            oacc[b, :, cols] = dot(takes[b], src)

    @pl.when(core == 0)
    def _():
        dz.wait_recv()
        total = part + zrecv[...].astype(F32)
        for i in range(2 * NX):
            fsend[i, 0:6, :] = total[i * 6 : (i + 1) * 6, :]
            fsend[i, 6:8, :] = jnp.zeros((2, QCOL), F32)
        mine = pltpu.make_async_copy(fsend.at[2 * px], frecv.at[px], loc_sem.at[11])
        mine.start()
        fins = [remote(fsend.at[2 * px + 1], frecv.at[px], fs.at[0, 1], fr.at[px],
                       dev(py, px, 1, pz))]
        for k in range(1, NX):
            to = mod(px + k, NX)
            for c in range(2):
                fins.append(
                    remote(fsend.at[2 * to + c], frecv.at[px], fs.at[k, c], fr.at[px],
                           dev(py, to, c, pz))
                )
        for c in fins:
            c.start()
        mine.wait()
        for k in range(1, NX):
            src = mod(px + k, NX)
            remote(fsend.at[0], frecv.at[src], fs.at[k, 0], fr.at[src],
                   dev(py, src, 0, pz)).wait_recv()
        for c in fins:
            c.wait_send()

    @pl.when(core == 1)
    def _():
        for src in range(NX):
            remote(fsend.at[0], frecv.at[src], fs.at[0, 0], fr.at[src],
                   dev(py, src, 0, pz)).wait_recv()
        dz.wait_send()

    for j in range(NX):
        for i in range(6):
            dgrad_ref[i, :, j * QCOL : (j + 1) * QCOL] = frecv[j, i : i + 1, :]

    takes = [taking(b, FAR, NEAR) for b in range(4)]
    self_back.wait()
    for e in src_near:
        back(*e, towards(e)).wait_recv()
    gsum = jnp.zeros((TOK, 1), F32)
    for n in range(4):
        cols = slice(n * 256, (n + 1) * 256)
        src = rrecv[FAR:, :, cols].reshape(NROWS, 256)
        for q in range(2):
            full = slice(q * HALF + n * 256, q * HALF + (n + 1) * 256)
            o = oacc[q, :, cols] + dot(takes[q], src)
            out_ref[:, full] = (gw_c * o).astype(BF16)
            gsum = gsum + jnp.sum(cot[:, full].astype(F32) * o, axis=1, keepdims=True)
            tgrad_ref[:, full] = (oacc[2 + q, :, cols] + dot(takes[2 + q], src)).astype(BF16)
    ggrad_ref[...] = jnp.sum(jnp.where(eye, gsum, 0.0), axis=0, keepdims=True)

    for c in outs + backs + dx_copies + merged + dy_copies:
        c.wait_send()


def hand_over(*refs):
    n = (len(refs) - 1) // 2
    copies = [
        pltpu.make_async_copy(refs[i], refs[n + i], refs[2 * n].at[i]) for i in range(n)
    ]
    for c in copies:
        c.start()
    for c in copies:
        c.wait()


def gathering(count, pad):
    perm = np.zeros((4 * pad, count * BLK), np.float32)
    for r in range(count * BLK):
        k, w = divmod(r, BLK)
        half, w = divmod(w, 2 * CAP)
        kind, s = divmod(w, CAP)
        perm[(kind * 2 + half) * pad + k * CAP + s, r] = 1.0
    return jnp.asarray(perm, BF16), jnp.asarray(perm.T, BF16)


def wanted():
    want = np.full((8, NZ * BLK), -1, np.int32)
    for r in range(NZ * BLK):
        k, w = divmod(r, BLK)
        half, w = divmod(w, 2 * CAP)
        kind, s = divmod(w, CAP)
        want[kind * 2 + half, r] = k * CAP + s
    return jnp.asarray(want)


def shards(tokens, expert_ids, gate_weights, cotangent, gate_weight, up_weight, down_weight):
    hbm = pl.BlockSpec(memory_space=pl.ANY)
    vmem = pl.BlockSpec(memory_space=pltpu.VMEM)
    dma = pltpu.SemaphoreType.DMA
    mem = pltpu.VMEM
    outs = (
        jax.ShapeDtypeStruct((TOK, WIDTH), BF16),
        jax.ShapeDtypeStruct((TOK, WIDTH), BF16),
        jax.ShapeDtypeStruct((1, TOK), F32),
        jax.ShapeDtypeStruct((FFW // (2 * NX * NY), 1, WIDTH), F32),
    )
    results = pl.pallas_call(
        kernel,
        out_shape=outs,
        in_specs=[hbm, hbm, vmem, vmem] + [hbm] * 7 + [vmem],
        out_specs=(vmem,) * 4,
        scratch_shapes=[
            mem((TOK, WIDTH), BF16), mem((TOK, WIDTH), BF16), mem((4 * TOK, HALF), BF16),
            mem((WIDTH, FFW), BF16), mem((WIDTH, FFW), BF16), mem((FFW, WIDTH), BF16),
            mem((4 * FPAD, FROWS), BF16), mem((FROWS, 4 * FPAD), BF16),
            mem((4 * NPAD, NROWS), BF16), mem((NROWS, 4 * NPAD), BF16),
            mem((NZ, BLK, HALF), BF16), mem((NZ, BLK, HALF), BF16),
            mem((4 * FPAD, HALF), BF16), mem((4 * FPAD, HALF), BF16),
            mem((4 * NPAD, HALF), BF16), mem((4 * NPAD, HALF), BF16),
            mem((NZ, BLK, HALF), BF16), mem((NZ, BLK, HALF), BF16),
            mem((4, TOK, HALF), F32),
            mem((NX, FFW, QCOL), F32), mem((NX, FFW, QCOL), BF16),
            mem((2, MID, QCOL), BF16), mem((2, MID, QCOL), BF16),
            mem((2, MID, QCOL), BF16), mem((2, MID, QCOL), BF16),
            mem((NY, DROWS, QCOL), F32), mem((NY, DROWS, QCOL), BF16),
            mem((NY - 1, DROWS, QCOL), BF16),
            mem((DROWS, QCOL), BF16), mem((DROWS, QCOL), BF16),
            mem((2 * NX, 8, QCOL), F32), mem((NX, 8, QCOL), F32),
            dma((12,)),
            dma((NZ,)), dma((NZ,)), dma((NZ,)), dma((NZ,)),
            dma((3,)), dma((3,)), dma((3,)), dma((3,)),
            dma((2, 4)), dma((2, 4)), dma((2, 2, 4)), dma((2, 2, 4)),
            dma((2, 2, 2)), dma((2, 2, 2)),
            dma((6,)), dma((6,)), dma((NY - 1,)), dma((NY - 1,)),
            dma((1,)), dma((1,)), dma((NX, 2)), dma((NX,)),
        ],
        compiler_params=pltpu.CompilerParams(
            collective_id=0, has_side_effects=True, vmem_limit_bytes=56 * 1024 * 1024
        ),
        cost_estimate=pl.CostEstimate(
            flops=6_000_000_000, bytes_accessed=16_000_000, transcendentals=100_000
        ),
    )(
        tokens, cotangent, expert_ids.reshape(1, TOK), gate_weights.reshape(1, TOK),
        gate_weight[0], up_weight[0], down_weight[0],
        *gathering(FAR, FPAD), *gathering(NEAR, NPAD), wanted(),
    )
    out, tgrad, ggrad, dgrad = pl.pallas_call(
        hand_over,
        out_shape=outs,
        in_specs=[hbm] * 4,
        out_specs=(hbm,) * 4,
        scratch_shapes=[dma((4,))],
        cost_estimate=pl.CostEstimate(flops=0, bytes_accessed=2_200_000, transcendentals=0),
    )(*results)
    return out, tgrad, ggrad.reshape(TOK, 1), jnp.transpose(dgrad, (1, 0, 2))


def solution(mesh):
    rows = P(("rep", "ep"), None)
    weight = P("ep", None, None)
    return jax.shard_map(
        shards,
        mesh=mesh,
        in_specs=(rows, rows, rows, rows, weight, weight, weight),
        out_specs=(rows, rows, rows, P("ep", "rep", None)),
        check_vma=False,
    )
```

time: 134 us -> 149 us (1.11)
  Pallas kernels: 125 us -> 148 us
  local copies, waits for them, and re-layouts: 8.45 us -> 0 us
    pallas_call x1 -> x2, Pallas kernels: 125 us -> 148 us  [the longest x1 113 us: shards(): pl.pallas_call(kernel, out_shape=outs, in_specs=[hbm, hbm, vmem, vmem] +...]
    unnamed x6 -> x0, local copies, waits for them, and re-layouts: 5.46 us -> none
    pallas_call x2 -> x0, local copies, waits for them, and re-layouts: 2.99 us -> none  [shards(): pl.pallas_call(kernel, out_shape=(jax.ShapeDtypeStruct((TOK, WIDTH), BF16...]
where the time goes in v2:
time: 149 us; the launch traced here: 148 us
  Pallas kernels  148 us (99%)
    pallas_call x1, Pallas kernels, shards(): pl.pallas_call(kernel, out_shape=outs, in_specs=[hbm, hbm, vmem, vmem] +...  113 us
    pallas_call x1, Pallas kernels, shards(): pl.pallas_call(hand_over, out_shape=outs, in_specs=[hbm] * 4, out_specs=(...  34.4 us

profile of v2, /device:TPU:1, one launch (start us, length us, event | category | flops | bytes accessed | tf_op | source)
XLA Modules:
  0.0 148.4 jit_solution(4370523276667737892)
XLA Ops:
  0.6 113.4 %shard_map.147 = (bf16[128,2048]{1,0:T(8,128)(2,1)}, bf16[128,2048]{1,0:T(8,128)(2,1)}, f32[1,128]{1,0:T(1,128)}, f32[6,1,2048]{2,1,0:T(1,128)}) custom-call(bf16[128,2048]{1,0:T(8,128)(2,1)} %x_hbm.1, bf16[128,2048]{1,0:T(8,128)(2,1)} %cot_hbm.1, s32[1,128]{1,0:T(1,128)} %bitcast.11, f32[1,128]{1,0:T(1,128)} %bitcast.12, bf16[2048,384]{1,0:T(8,128)(2,1)} %bitcast.7, ...), custom_call_target="tpu_custom_call" | custom-call | flops 6000000000 | bytes 16000000 | tf_op jit(solution)/shard_map/pallas_call | solution.py:533
  114.0 34.4 %shard_map.148 = (bf16[128,2048]{1,0:T(8,128)(2,1)}, bf16[128,2048]{1,0:T(8,128)(2,1)}, f32[1,128]{1,0:T(1,128)}, f32[6,1,2048]{2,1,0:T(1,128)}) custom-call(bf16[128,2048]{1,0:T(8,128)(2,1)} %get-tuple-element.12.refs_0_, bf16[128,2048]{1,0:T(8,128)(2,1)} %get-tuple-element.13.refs_1_, f32[1,128]{1,0:T(1,128)} %get-tuple-element.14.refs_2_, ...), custom_call_target="tpu_custom_call" | custom-call | bytes 2200000 | tf_op jit(solution)/shard_map/pallas_call | solution.py:574

commit v3 on v2

--- a/solution.py
+++ b/solution.py
@@ -19,6 +19,7 @@
 DROWS = FFW // NY
 QCOL = WIDTH // NX
 MID = FFW // 2
+GCOL = QCOL // 2
 MESH = pl.DeviceIdType.MESH
 F32 = jnp.float32
 BF16 = jnp.bfloat16
@@ -147,6 +148,17 @@
     z[2 * TOK : 3 * TOK, :] = dout[:, :HALF]
     z[3 * TOK :, :] = dout[:, HALF:]
 
+    def build(first, count):
+        place = placing(first, count)
+
+        @pl.loop(0, 4)
+        def _(n):
+            cols = ds(n * 256, 256)
+            send[first : first + count, :, cols] = (
+                dot(place, z[:, cols]).astype(BF16).reshape(count, BLK, 256)
+            )
+
+    build(0, FAR)
     pl.semaphore_wait(barrier, len(peers))
 
     own = (
@@ -202,21 +214,14 @@
     src_far, src_near = as_source()
     exp_far, exp_near = as_expert()
 
-    outs = []
-    for first, count, group in ((0, FAR, src_far), (FAR, NEAR, src_near)):
-        place = placing(first, count)
-
-        @pl.loop(0, 4)
-        def _(n):
-            cols = ds(n * 256, 256)
-            send[first : first + count, :, cols] = (
-                dot(place, z[:, cols]).astype(BF16).reshape(count, BLK, 256)
-            )
-
-        for e in group:
-            c = there(*e, towards(e))
-            c.start()
-            outs.append(c)
+    outs = [there(*e, towards(e)) for e in src_far]
+    for c in outs:
+        c.start()
+    build(FAR, NEAR)
+    for e in src_near:
+        c = there(*e, towards(e))
+        c.start()
+        outs.append(c)
     self_out = pltpu.make_async_copy(send.at[mine_q], recv.at[mine_k], loc_sem.at[9])
     self_out.start()
 
@@ -341,14 +346,13 @@
         there(*e, whence(e)).wait_recv()
     hf_far, da, db = gather_rows(0, FAR, FPAD, pf, xf)
     results(0, FAR, FPAD, pft, yf, hf_far, da, db)
+    self_out.wait()
+    for e in exp_near:
+        there(*e, whence(e)).wait_recv()
     for e in exp_far:
         c = back(*e, whence(e))
         c.start()
         backs.append(c)
-
-    self_out.wait()
-    for e in exp_near:
-        there(*e, whence(e)).wait_recv()
     hf, da, db = gather_rows(FAR, NEAR, NPAD, pn, xn)
 
     htf = jnp.transpose(hf_far).astype(BF16)
@@ -358,17 +362,19 @@
         piece = dot(htf, xf[q * FPAD : (q + 1) * FPAD, c0 : c0 + QCOL])
         piece = piece + dot(htn, xn[q * NPAD : (q + 1) * NPAD, c0 : c0 + QCOL])
         dw[j] = piece
-        dwb[j] = piece.astype(BF16)
+        for g in range(2):
+            dwb[g, j] = piece[:, g * GCOL : (g + 1) * GCOL].astype(BF16)
     right, left, across = mod(px + 1, NX), mod(px - 1, NX), mod(px + 2, NX)
     lo, hi = slice(0, MID), slice(MID, FFW)
-    dx_copies = [
-        remote(dwb.at[across, lo], opp.at[0], dxs.at[0], dxr.at[0], at_x(1)),
-        remote(dwb.at[across, hi], opp.at[1], dxs.at[1], dxr.at[1], at_x(-1)),
-        remote(dwb.at[right, hi], pure.at[0], dxs.at[2], dxr.at[2], at_x(1)),
-        remote(dwb.at[left, lo], pure.at[1], dxs.at[3], dxr.at[3], at_x(-1)),
-    ]
-    for c in dx_copies:
-        c.start()
+    dx_copies = []
+    for g in range(2):
+        for i, (to, rr, side) in enumerate(
+            ((across, lo, 1), (across, hi, -1), (right, hi, 1), (left, lo, -1))
+        ):
+            dst = (opp if i < 2 else pure).at[g, i % 2]
+            c = remote(dwb.at[g, to, rr], dst, dxs.at[g, i], dxr.at[g, i], at_x(side))
+            c.start()
+            dx_copies.append(c)
 
     results(FAR, NEAR, NPAD, pnt, yn, hf, da, db)
     for e in exp_near:
@@ -378,37 +384,44 @@
     self_back = pltpu.make_async_copy(rsend.at[mine_k], rrecv.at[mine_q], loc_sem.at[10])
     self_back.start()
 
-    merged = [
-        remote(msend.at[0], mrecv.at[0], dxs.at[4], dxr.at[4], at_x(1)),
-        remote(msend.at[1], mrecv.at[1], dxs.at[5], dxr.at[5], at_x(-1)),
-    ]
-    dx_copies[0].wait_recv()
-    msend[0] = (dw[right, lo, :] + opp[0].astype(F32)).astype(BF16)
-    merged[0].start()
-    dx_copies[1].wait_recv()
-    msend[1] = (dw[left, hi, :] + opp[1].astype(F32)).astype(BF16)
-    merged[1].start()
-    for c in dx_copies[2:] + merged:
-        c.wait_recv()
-    for i in range(NY):
-        top = i < NY // 2
-        rr = slice(i * DROWS, (i + 1) * DROWS)
-        r0 = i * DROWS - (0 if top else MID)
-        rm = slice(r0, r0 + DROWS)
-        m, p = (0, 1) if top else (1, 0)
-        part = dw[px, rr, :] + mrecv[m, rm, :].astype(F32) + pure[p, rm, :].astype(F32)
-        ysum[i] = part
-        yb[i] = part.astype(BF16)
+    halves = [slice(g * GCOL, (g + 1) * GCOL) for g in range(2)]
+    merged = []
+    for g in range(2):
+        for i, (to, rr, side) in enumerate(((right, lo, 1), (left, hi, -1))):
+            dx_copies[4 * g + i].wait_recv()
+            msend[g, i] = (dw[to, rr, halves[g]] + opp[g, i].astype(F32)).astype(BF16)
+            c = remote(msend.at[g, i], mrecv.at[g, i], dxs.at[g, 4 + i], dxr.at[g, 4 + i],
+                       at_x(side))
+            c.start()
+            merged.append(c)
     dy_copies = []
-    for k in (4, 3, 5, 2, 6, 1, 7):
-        c = remote(yb.at[mod(py + k, NY)], yrecv.at[k - 1], dys.at[k - 1], dyr.at[k - 1], at_y(k))
-        c.start()
-        dy_copies.append(c)
-    for c in dy_copies:
-        c.wait_recv()
-    part = ysum[py]
-    for k in range(NY - 1):
-        part = part + yrecv[k].astype(F32)
+    for g in range(2):
+        for c in dx_copies[4 * g + 2 : 4 * g + 4] + merged[2 * g : 2 * g + 2]:
+            c.wait_recv()
+        for i in range(NY):
+            top = i < NY // 2
+            rr = slice(i * DROWS, (i + 1) * DROWS)
+            r0 = i * DROWS - (0 if top else MID)
+            rm = slice(r0, r0 + DROWS)
+            m, p = (0, 1) if top else (1, 0)
+            got = mrecv[g, m, rm, :].astype(F32) + pure[g, p, rm, :].astype(F32)
+            got = dw[px, rr, halves[g]] + got
+            ysum[i, :, halves[g]] = got
+            yb[g, i] = got.astype(BF16)
+        for k in (4, 3, 5, 2, 6, 1, 7):
+            c = remote(yb.at[g, mod(py + k, NY)], yrecv.at[g, k - 1], dys.at[g, k - 1],
+                       dyr.at[g, k - 1], at_y(k))
+            c.start()
+            dy_copies.append(c)
+    sums = []
+    for g in range(2):
+        for c in dy_copies[g * (NY - 1) : (g + 1) * (NY - 1)]:
+            c.wait_recv()
+        got = ysum[py, :, halves[g]]
+        for k in range(NY - 1):
+            got = got + yrecv[g, k].astype(F32)
+        sums.append(got)
+    part = jnp.concatenate(sums, axis=1)
     zsend[...] = part.astype(BF16)
     dz = remote(zsend, zrecv, dzs.at[0], dzr.at[0], at_z(8, other))
 
@@ -489,14 +502,9 @@
 
 
 def hand_over(*refs):
-    n = (len(refs) - 1) // 2
-    copies = [
-        pltpu.make_async_copy(refs[i], refs[n + i], refs[2 * n].at[i]) for i in range(n)
-    ]
-    for c in copies:
-        c.start()
-    for c in copies:
-        c.wait()
+    n = len(refs) // 2
+    for i in range(n):
+        refs[n + i][...] = refs[i][...]
 
 
 def gathering(count, pad):
@@ -545,11 +553,11 @@
             mem((4 * NPAD, HALF), BF16), mem((4 * NPAD, HALF), BF16),
             mem((NZ, BLK, HALF), BF16), mem((NZ, BLK, HALF), BF16),
             mem((4, TOK, HALF), F32),
-            mem((NX, FFW, QCOL), F32), mem((NX, FFW, QCOL), BF16),
-            mem((2, MID, QCOL), BF16), mem((2, MID, QCOL), BF16),
-            mem((2, MID, QCOL), BF16), mem((2, MID, QCOL), BF16),
-            mem((NY, DROWS, QCOL), F32), mem((NY, DROWS, QCOL), BF16),
-            mem((NY - 1, DROWS, QCOL), BF16),
+            mem((NX, FFW, QCOL), F32), mem((2, NX, FFW, GCOL), BF16),
+            mem((2, 2, MID, GCOL), BF16), mem((2, 2, MID, GCOL), BF16),
+            mem((2, 2, MID, GCOL), BF16), mem((2, 2, MID, GCOL), BF16),
+            mem((NY, DROWS, QCOL), F32), mem((2, NY, DROWS, GCOL), BF16),
+            mem((2, NY - 1, DROWS, GCOL), BF16),
             mem((DROWS, QCOL), BF16), mem((DROWS, QCOL), BF16),
             mem((2 * NX, 8, QCOL), F32), mem((NX, 8, QCOL), F32),
             dma((12,)),
@@ -557,7 +565,7 @@
             dma((3,)), dma((3,)), dma((3,)), dma((3,)),
             dma((2, 4)), dma((2, 4)), dma((2, 2, 4)), dma((2, 2, 4)),
             dma((2, 2, 2)), dma((2, 2, 2)),
-            dma((6,)), dma((6,)), dma((NY - 1,)), dma((NY - 1,)),
+            dma((2, 6)), dma((2, 6)), dma((2, NY - 1)), dma((2, NY - 1)),
             dma((1,)), dma((1,)), dma((NX, 2)), dma((NX,)),
         ],
         compiler_params=pltpu.CompilerParams(
@@ -574,9 +582,8 @@
     out, tgrad, ggrad, dgrad = pl.pallas_call(
         hand_over,
         out_shape=outs,
-        in_specs=[hbm] * 4,
-        out_specs=(hbm,) * 4,
-        scratch_shapes=[dma((4,))],
+        in_specs=[vmem] * 4,
+        out_specs=(vmem,) * 4,
         cost_estimate=pl.CostEstimate(flops=0, bytes_accessed=2_200_000, transcendentals=0),
     )(*results)
     return out, tgrad, ggrad.reshape(TOK, 1), jnp.transpose(dgrad, (1, 0, 2))

time: 149 us -> 118 us (0.79)
  Pallas kernels: 148 us -> 117 us
    pallas_call x1, Pallas kernels: 34.4 us -> 2.21 us  [shards(): pl.pallas_call(hand_over, out_shape=outs, in_specs=[vmem] * 4, out_specs=...]
where the time goes in v3:
time: 118 us; the launch traced here: 117 us
  Pallas kernels  117 us (99%)
    pallas_call x1, Pallas kernels, shards(): pl.pallas_call(kernel, out_shape=outs, in_specs=[hbm, hbm, vmem, vmem] +...  115 us

profile of v3, /device:TPU:1, one launch (start us, length us, event | category | flops | bytes accessed | tf_op | source)
XLA Modules:
  0.0 117.4 jit_solution(5064085074368412707)
XLA Ops:
  0.6 114.5 %shard_map.147 = (bf16[128,2048]{1,0:T(8,128)(2,1)}, bf16[128,2048]{1,0:T(8,128)(2,1)}, f32[1,128]{1,0:T(1,128)}, f32[6,1,2048]{2,1,0:T(1,128)}) custom-call(bf16[128,2048]{1,0:T(8,128)(2,1)} %x_hbm.1, bf16[128,2048]{1,0:T(8,128)(2,1)} %cot_hbm.1, s32[1,128]{1,0:T(1,128)} %bitcast.11, f32[1,128]{1,0:T(1,128)} %bitcast.12, bf16[2048,384]{1,0:T(8,128)(2,1)} %bitcast.7, ...), custom_call_target="tpu_custom_call" | custom-call | flops 6000000000 | bytes 16000000 | tf_op jit(solution)/shard_map/pallas_call | solution.py:541
  115.2 2.2 %shard_map.148 = (bf16[128,2048]{1,0:T(8,128)(2,1)}, bf16[128,2048]{1,0:T(8,128)(2,1)}, f32[1,128]{1,0:T(1,128)}, f32[6,1,2048]{2,1,0:T(1,128)}) custom-call(bf16[128,2048]{1,0:T(8,128)(2,1)} %get-tuple-element.12.refs_0_, bf16[128,2048]{1,0:T(8,128)(2,1)} %get-tuple-element.13.refs_1_, f32[1,128]{1,0:T(1,128)} %get-tuple-element.14.refs_2_, ...), custom_call_target="tpu_custom_call" | custom-call | bytes 2200000 | tf_op jit(solution)/shard_map/pallas_call | solution.py:582

commit v4 on v3

--- a/solution.py
+++ b/solution.py
@@ -46,7 +46,7 @@
     x, cot, z, wg, wu, wd, pf, pft, pn, pnt, send, recv, xf, yf, xn, yn, rsend, rrecv,
     oacc, dw, dwb, opp, pure, msend, mrecv, ysum, yb, yrecv, zsend, zrecv, fsend, frecv,
     loc_sem, s1, r1, s2, r2, wzs, wzr, gxs, gxr, gys, gyr, uys, uyr, uxs, uxr,
-    dxs, dxr, dys, dyr, dzs, dzr, fs, fr,
+    dxs, dxr, dys, dyr, dzs, dzr, fs, fr, go_sem,
 ):
     rep = lax.axis_index("rep")
     pz = lax.axis_index("ep")
@@ -140,25 +140,7 @@
             axis=1,
         )
 
-    for c in loads:
-        c.wait()
-    z[0:TOK, :] = x[:, :HALF]
-    z[TOK : 2 * TOK, :] = x[:, HALF:]
-    dout = (gw_c * cot[...].astype(F32)).astype(BF16)
-    z[2 * TOK : 3 * TOK, :] = dout[:, :HALF]
-    z[3 * TOK :, :] = dout[:, HALF:]
-
-    def build(first, count):
-        place = placing(first, count)
-
-        @pl.loop(0, 4)
-        def _(n):
-            cols = ds(n * 256, 256)
-            send[first : first + count, :, cols] = (
-                dot(place, z[:, cols]).astype(BF16).reshape(count, BLK, 256)
-            )
-
-    build(0, FAR)
+    place_far = placing(0, FAR)
     pl.semaphore_wait(barrier, len(peers))
 
     own = (
@@ -175,6 +157,24 @@
     def _():
         for m in (1, 2, 0):
             wz[m].start()
+
+    for c in loads[:2]:
+        c.wait()
+    z[0:TOK, :] = x[:, :HALF]
+    z[TOK : 2 * TOK, :] = x[:, HALF:]
+    dout = (gw_c * cot[...].astype(F32)).astype(BF16)
+    z[2 * TOK : 3 * TOK, :] = dout[:, :HALF]
+    z[3 * TOK :, :] = dout[:, HALF:]
+
+    def build(place, first, count):
+        @pl.loop(0, 4)
+        def _(n):
+            cols = ds(n * 256, 256)
+            send[first : first + count, :, cols] = (
+                dot(place, z[:, cols]).astype(BF16).reshape(count, BLK, 256)
+            )
+
+    build(place_far, 0, FAR)
 
     def as_source():
         far = [(tie, core, 1, 4 + core), (tie, other, 4, 4 + core)]
@@ -217,7 +217,37 @@
     outs = [there(*e, towards(e)) for e in src_far]
     for c in outs:
         c.start()
-    build(FAR, NEAR)
+    build(placing(FAR, NEAR), FAR, NEAR)
+
+    def y_slice(m, y):
+        if m == 0:
+            return wg.at[ds(y * (NX * GROWS), NX * GROWS), ALL]
+        if m == 1:
+            return wu.at[ds(px * (NY * GROWS) + y * GROWS, GROWS), ALL]
+        return wd.at[ds(y * DROWS, DROWS), ds(px * QCOL, QCOL)]
+
+    def first_copies(m):
+        if m == 0:
+            w = wg.at[own[0]]
+            return [remote(w, w, gxs.at[k - 1], gxr.at[k - 1], at_x(k)) for k in (2, 1, 3)]
+        w = y_slice(m, py)
+        return [
+            remote(w, w, uys.at[m - 1, k - 1], uyr.at[m - 1, k - 1], at_y(k))
+            for k in (4, 3, 5, 2, 6, 1, 7)
+        ]
+
+    @pl.when(core == 1)
+    def _():
+        for m in (1, 2, 0):
+            wz[m].wait_recv()
+            for c in first_copies(m):
+                c.start()
+        pl.semaphore_signal(go_sem, inc=1, device_id=at_z(0, other), device_id_type=MESH)
+
+    @pl.when(core == 0)
+    def _():
+        pl.semaphore_wait(go_sem, 1)
+
     for e in src_near:
         c = there(*e, towards(e))
         c.start()
@@ -227,77 +257,75 @@
 
     @pl.when(core == 1)
     def _():
-        started = list(wz)
+        started = wz + first_copies(0) + first_copies(1) + first_copies(2)
 
         def go(c):
             c.start()
             started.append(c)
 
-        def y_slice(m, y):
-            if m == 0:
-                return wg.at[ds(y * (NX * GROWS), NX * GROWS), ALL]
-            if m == 1:
-                return wu.at[ds(px * (NY * GROWS) + y * GROWS, GROWS), ALL]
-            return wd.at[ds(y * DROWS, DROWS), ds(px * QCOL, QCOL)]
-
-        depth = ((4, 3), (3, 4), (3, 4))
-
-        def chain(m, step):
-            ss, rs = (gys, gyr) if m == 0 else (uys.at[m - 1], uyr.at[m - 1])
-            for side, sign in ((0, 1), (1, -1)):
-                if step > depth[m][side]:
-                    continue
-                w = y_slice(m, mod(py - sign * step, NY))
+        sides = ((0, 1), (1, -1))
+
+        def chain(step):
+            for side, sign in sides:
+                w = y_slice(0, mod(py - sign * step, NY))
+                if step == 4:
+                    w = w.at[half_rows[side]]
                 if step > 0:
-                    remote(w, w, ss.at[side, step - 1], rs.at[side, step - 1],
+                    remote(w, w, gys.at[side, step - 1], gyr.at[side, step - 1],
                            at_y(sign)).wait_recv()
-                if step < depth[m][side]:
-                    go(remote(w, w, ss.at[side, step], rs.at[side, step], at_y(sign)))
-
-        def x_block(m, xx, part=None):
+                if step == 3:
+                    w = w.at[half_rows[side]]
+                if step < 4:
+                    go(remote(w, w, gys.at[side, step], gyr.at[side, step], at_y(sign)))
+
+        half_rows = [slice(i * (GROWS * NX // 2), (i + 1) * (GROWS * NX // 2)) for i in range(2)]
+
+        def x_part(m, xx, part):
             if m == 1:
                 n = NY * GROWS
-                if part is None:
-                    return wu.at[ds(xx * n, n), ALL]
                 return wu.at[ds(xx * n + part * (n // 2), n // 2), ALL]
-            rows = ALL if part is None else slice(part * MID, (part + 1) * MID)
-            return wd.at[rows, ds(xx * QCOL, QCOL)]
-
-        for m in (1, 2):
-            wz[m].wait_recv()
-            chain(m, 0)
-        wz[0].wait_recv()
-        w = wg.at[own[0]]
-        for k in (2, 1, 3):
-            go(remote(w, w, gxs.at[k - 1], gxr.at[k - 1], at_x(k)))
-        for m in (1, 2):
-            chain(m, 1)
+            return wd.at[part * MID : (part + 1) * MID, ds(xx * QCOL, QCOL)]
+
+        def from_y(m):
+            for k in (1, 7, 2, 6, 3, 5, 4):
+                w = y_slice(m, mod(py - k, NY))
+                remote(w, w, uys.at[m - 1, k - 1], uyr.at[m - 1, k - 1], at_y(k)).wait_recv()
+
+        def x_copy(m, side, sign, i, hops):
+            w = x_part(m, mod(px - sign * hops, NX), side if i != 1 else 1 - side)
+            return remote(w, w, uxs.at[m - 1, side, i], uxr.at[m - 1, side, i], at_x(sign))
+
+        def along_x(m):
+            for i in range(2):
+                for side, sign in sides:
+                    go(x_copy(m, side, sign, i, 0))
+
+        def forward_x(m):
+            for side, sign in sides:
+                x_copy(m, side, sign, 0, 1).wait_recv()
+                go(x_copy(m, side, sign, 2, 1))
+
+        def from_x(m):
+            for side, sign in sides:
+                x_copy(m, side, sign, 1, 1).wait_recv()
+                x_copy(m, side, sign, 2, 2).wait_recv()
+
         for k in (1, 3, 2):
             w = wg.at[ds(py * (NX * GROWS) + mod(px - k, NX) * GROWS, GROWS), ALL]
             remote(w, w, gxs.at[k - 1], gxr.at[k - 1], at_x(k)).wait_recv()
-        chain(0, 0)
-        for step in (2, 3, 4):
-            for m in (1, 2):
-                chain(m, step)
-        for m in (1, 2):
-            w = x_block(m, px)
-            for side, sign in ((0, 1), (1, -1)):
-                go(remote(w, w, uxs.at[m - 1, side, 0], uxr.at[m - 1, side, 0], at_x(sign)))
-        chain(0, 1)
-        for m in (1, 2):
-            for side, sign in ((0, 1), (1, -1)):
-                w = x_block(m, mod(px - sign, NX))
-                remote(w, w, uxs.at[m - 1, side, 0], uxr.at[m - 1, side, 0],
-                       at_x(sign)).wait_recv()
-                w = x_block(m, mod(px - sign, NX), side)
-                go(remote(w, w, uxs.at[m - 1, side, 1], uxr.at[m - 1, side, 1], at_x(sign)))
-        for step in (2, 3, 4):
-            chain(0, step)
-        for m in (1, 2):
-            for side, sign in ((0, 1), (1, -1)):
-                w = x_block(m, mod(px + 2, NX), side)
-                remote(w, w, uxs.at[m - 1, side, 1], uxr.at[m - 1, side, 1],
-                       at_x(sign)).wait_recv()
+        chain(0)
+        from_y(1)
+        along_x(1)
+        chain(1)
+        from_y(2)
+        along_x(2)
+        forward_x(1)
+        chain(2)
+        forward_x(2)
+        chain(3)
+        from_x(1)
+        chain(4)
+        from_x(2)
         for c in started:
             c.wait_send()
 
@@ -341,6 +369,8 @@
                 dot(perm_t[...], src[:, cols]).astype(BF16).reshape(count, BLK, 256)
             )
 
+    for c in loads[2:]:
+        c.wait()
     backs = []
     for e in exp_far:
         there(*e, whence(e)).wait_recv()
@@ -377,7 +407,7 @@
             dx_copies.append(c)
 
     results(FAR, NEAR, NPAD, pnt, yn, hf, da, db)
-    for e in exp_near:
+    for e in exp_near[:4]:
         c = back(*e, whence(e))
         c.start()
         backs.append(c)
@@ -429,6 +459,11 @@
     def _():
         dz.start()
 
+    for e in exp_near[4:]:
+        c = back(*e, whence(e))
+        c.start()
+        backs.append(c)
+
     def taking(b, first, count):
         rows = slice(first * BLK, (first + count) * BLK)
         return jnp.where(wantc[b : b + 1, rows] == tgt_c, 1.0, 0.0).astype(BF16)
@@ -563,10 +598,10 @@
             dma((12,)),
             dma((NZ,)), dma((NZ,)), dma((NZ,)), dma((NZ,)),
             dma((3,)), dma((3,)), dma((3,)), dma((3,)),
-            dma((2, 4)), dma((2, 4)), dma((2, 2, 4)), dma((2, 2, 4)),
-            dma((2, 2, 2)), dma((2, 2, 2)),
+            dma((2, 4)), dma((2, 4)), dma((2, NY - 1)), dma((2, NY - 1)),
+            dma((2, 2, 3)), dma((2, 2, 3)),
             dma((2, 6)), dma((2, 6)), dma((2, NY - 1)), dma((2, NY - 1)),
-            dma((1,)), dma((1,)), dma((NX, 2)), dma((NX,)),
+            dma((1,)), dma((1,)), dma((NX, 2)), dma((NX,)), pltpu.SemaphoreType.REGULAR,
         ],
         compiler_params=pltpu.CompilerParams(
             collective_id=0, has_side_effects=True, vmem_limit_bytes=56 * 1024 * 1024

time: 118 us -> 115 us (0.975)
  Pallas kernels: 117 us -> 114 us
    pallas_call x1, Pallas kernels: 115 us -> 112 us  [shards(): pl.pallas_call(kernel, out_shape=outs, in_specs=[hbm, hbm, vmem, vmem] +...]
where the time goes in v4:
time: 115 us
  Pallas kernels  114 us (99%)
    pallas_call x1, Pallas kernels, shards(): pl.pallas_call(kernel, out_shape=outs, in_specs=[hbm, hbm, vmem, vmem] +...  112 us

profile of v4, /device:TPU:1, one launch (start us, length us, event | category | flops | bytes accessed | tf_op | source)
XLA Modules:
  0.0 114.8 jit_solution(10104439271931350724)
XLA Ops:
  0.6 111.9 %shard_map.147 = (bf16[128,2048]{1,0:T(8,128)(2,1)}, bf16[128,2048]{1,0:T(8,128)(2,1)}, f32[1,128]{1,0:T(1,128)}, f32[6,1,2048]{2,1,0:T(1,128)}) custom-call(bf16[128,2048]{1,0:T(8,128)(2,1)} %x_hbm.1, bf16[128,2048]{1,0:T(8,128)(2,1)} %cot_hbm.1, s32[1,128]{1,0:T(1,128)} %bitcast.11, f32[1,128]{1,0:T(1,128)} %bitcast.12, bf16[2048,384]{1,0:T(8,128)(2,1)} %bitcast.7, ...), custom_call_target="tpu_custom_call" | custom-call | flops 6000000000 | bytes 16000000 | tf_op jit(solution)/shard_map/pallas_call | solution.py:576
  112.6 2.2 %shard_map.148 = (bf16[128,2048]{1,0:T(8,128)(2,1)}, bf16[128,2048]{1,0:T(8,128)(2,1)}, f32[1,128]{1,0:T(1,128)}, f32[6,1,2048]{2,1,0:T(1,128)}) custom-call(bf16[128,2048]{1,0:T(8,128)(2,1)} %get-tuple-element.12.refs_0_, bf16[128,2048]{1,0:T(8,128)(2,1)} %get-tuple-element.13.refs_1_, f32[1,128]{1,0:T(1,128)} %get-tuple-element.14.refs_2_, ...), custom_call_target="tpu_custom_call" | custom-call | bytes 2200000 | tf_op jit(solution)/shard_map/pallas_call | solution.py:617

commit v5 on v4

--- a/solution.py
+++ b/solution.py
@@ -78,13 +78,15 @@
 
     tie, tie_other = 4 - 8 * core, 4 - 8 * other
     barrier = pltpu.get_barrier_semaphore()
-    peers = [at_z(o, core) for o in (-4, -3, -2, -1, 1, 2, 3, 4, 8)]
-    peers += [at_z(o, other) for o in (-3, -2, -1, 0, 1, 2, 3, 8)] + [at_z(tie, other)]
-    for k in range(1, NX):
+    peers = [at_z(8, core), at_z(8, other), at_z(-4, core), at_z(4, core), at_z(tie, other)]
+    for k in (4, 3, 5, 2, 6, 1, 7):
+        peers.append(at_y(k))
+    for o in (-3, 3, -2, 2, -1, 1):
+        peers += [at_z(o, core), at_z(o, other)]
+    for k in (2, 1, 3):
         peers.append(at_x(k))
         peers.append(dev(py, mod(px + k, NX), other, pz))
-    for k in range(1, NY):
-        peers.append(at_y(k))
+    peers.append(at_z(0, other))
     for peer in peers:
         pl.semaphore_signal(barrier, inc=1, device_id=peer, device_id_type=MESH)
 
@@ -374,15 +376,21 @@
     backs = []
     for e in exp_far:
         there(*e, whence(e)).wait_recv()
-    hf_far, da, db = gather_rows(0, FAR, FPAD, pf, xf)
-    results(0, FAR, FPAD, pft, yf, hf_far, da, db)
+    hf_far, da_far, db_far = gather_rows(0, FAR, FPAD, pf, xf)
+
+    @pl.when(core == 0)
+    def _():
+        results(0, FAR, FPAD, pft, yf, hf_far, da_far, db_far)
+
     self_out.wait()
     for e in exp_near:
         there(*e, whence(e)).wait_recv()
-    for e in exp_far:
-        c = back(*e, whence(e))
-        c.start()
-        backs.append(c)
+
+    @pl.when(core == 0)
+    def _():
+        for e in exp_far:
+            back(*e, whence(e)).start()
+
     hf, da, db = gather_rows(FAR, NEAR, NPAD, pn, xn)
 
     htf = jnp.transpose(hf_far).astype(BF16)
@@ -406,8 +414,15 @@
             c.start()
             dx_copies.append(c)
 
+    @pl.when(core == 1)
+    def _():
+        results(0, FAR, FPAD, pft, yf, hf_far, da_far, db_far)
+        for e in exp_far:
+            back(*e, whence(e)).start()
+
+    backs += [back(*e, whence(e)) for e in exp_far]
     results(FAR, NEAR, NPAD, pnt, yn, hf, da, db)
-    for e in exp_near[:4]:
+    for e in exp_near[0:3:2]:
         c = back(*e, whence(e))
         c.start()
         backs.append(c)
@@ -443,7 +458,7 @@
                        dyr.at[g, k - 1], at_y(k))
             c.start()
             dy_copies.append(c)
-    sums = []
+    sums, dz = [], []
     for g in range(2):
         for c in dy_copies[g * (NY - 1) : (g + 1) * (NY - 1)]:
             c.wait_recv()
@@ -451,15 +466,15 @@
         for k in range(NY - 1):
             got = got + yrecv[g, k].astype(F32)
         sums.append(got)
-    part = jnp.concatenate(sums, axis=1)
-    zsend[...] = part.astype(BF16)
-    dz = remote(zsend, zrecv, dzs.at[0], dzr.at[0], at_z(8, other))
-
-    @pl.when(core == 1)
-    def _():
-        dz.start()
-
-    for e in exp_near[4:]:
+        zsend[g] = got.astype(BF16)
+        c = remote(zsend.at[g], zrecv.at[g], dzs.at[g], dzr.at[g], at_z(8, other))
+        dz.append(c)
+
+        @pl.when(core == 1)
+        def _():
+            c.start()
+
+    for e in exp_near[1:4:2] + exp_near[4:]:
         c = back(*e, whence(e))
         c.start()
         backs.append(c)
@@ -477,15 +492,7 @@
         for b in range(4):
             oacc[b, :, cols] = dot(takes[b], src)
 
-    @pl.when(core == 0)
-    def _():
-        dz.wait_recv()
-        total = part + zrecv[...].astype(F32)
-        for i in range(2 * NX):
-            fsend[i, 0:6, :] = total[i * 6 : (i + 1) * 6, :]
-            fsend[i, 6:8, :] = jnp.zeros((2, QCOL), F32)
-        mine = pltpu.make_async_copy(fsend.at[2 * px], frecv.at[px], loc_sem.at[11])
-        mine.start()
+    def fin_copies():
         fins = [remote(fsend.at[2 * px + 1], frecv.at[px], fs.at[0, 1], fr.at[px],
                        dev(py, px, 1, pz))]
         for k in range(1, NX):
@@ -495,26 +502,23 @@
                     remote(fsend.at[2 * to + c], frecv.at[px], fs.at[k, c], fr.at[px],
                            dev(py, to, c, pz))
                 )
-        for c in fins:
+        return fins
+
+    mine = pltpu.make_async_copy(fsend.at[2 * px], frecv.at[px], loc_sem.at[11])
+
+    @pl.when(core == 0)
+    def _():
+        total = []
+        for g in range(2):
+            dz[g].wait_recv()
+            total.append(sums[g] + zrecv[g].astype(F32))
+        total = jnp.concatenate(total, axis=1)
+        for i in range(2 * NX):
+            fsend[i, 0:6, :] = total[i * 6 : (i + 1) * 6, :]
+            fsend[i, 6:8, :] = jnp.zeros((2, QCOL), F32)
+        mine.start()
+        for c in fin_copies():
             c.start()
-        mine.wait()
-        for k in range(1, NX):
-            src = mod(px + k, NX)
-            remote(fsend.at[0], frecv.at[src], fs.at[k, 0], fr.at[src],
-                   dev(py, src, 0, pz)).wait_recv()
-        for c in fins:
-            c.wait_send()
-
-    @pl.when(core == 1)
-    def _():
-        for src in range(NX):
-            remote(fsend.at[0], frecv.at[src], fs.at[0, 0], fr.at[src],
-                   dev(py, src, 0, pz)).wait_recv()
-        dz.wait_send()
-
-    for j in range(NX):
-        for i in range(6):
-            dgrad_ref[i, :, j * QCOL : (j + 1) * QCOL] = frecv[j, i : i + 1, :]
 
     takes = [taking(b, FAR, NEAR) for b in range(4)]
     self_back.wait()
@@ -531,6 +535,28 @@
             gsum = gsum + jnp.sum(cot[:, full].astype(F32) * o, axis=1, keepdims=True)
             tgrad_ref[:, full] = (oacc[2 + q, :, cols] + dot(takes[2 + q], src)).astype(BF16)
     ggrad_ref[...] = jnp.sum(jnp.where(eye, gsum, 0.0), axis=0, keepdims=True)
+
+    @pl.when(core == 0)
+    def _():
+        mine.wait()
+        for k in range(1, NX):
+            src = mod(px + k, NX)
+            remote(fsend.at[0], frecv.at[src], fs.at[k, 0], fr.at[src],
+                   dev(py, src, 0, pz)).wait_recv()
+        for c in fin_copies():
+            c.wait_send()
+
+    @pl.when(core == 1)
+    def _():
+        for src in range(NX):
+            remote(fsend.at[0], frecv.at[src], fs.at[0, 0], fr.at[src],
+                   dev(py, src, 0, pz)).wait_recv()
+        for c in dz:
+            c.wait_send()
+
+    for j in range(NX):
+        for i in range(6):
+            dgrad_ref[i, :, j * QCOL : (j + 1) * QCOL] = frecv[j, i : i + 1, :]
 
     for c in outs + backs + dx_copies + merged + dy_copies:
         c.wait_send()
@@ -593,7 +619,7 @@
             mem((2, 2, MID, GCOL), BF16), mem((2, 2, MID, GCOL), BF16),
             mem((NY, DROWS, QCOL), F32), mem((2, NY, DROWS, GCOL), BF16),
             mem((2, NY - 1, DROWS, GCOL), BF16),
-            mem((DROWS, QCOL), BF16), mem((DROWS, QCOL), BF16),
+            mem((2, DROWS, GCOL), BF16), mem((2, DROWS, GCOL), BF16),
             mem((2 * NX, 8, QCOL), F32), mem((NX, 8, QCOL), F32),
             dma((12,)),
             dma((NZ,)), dma((NZ,)), dma((NZ,)), dma((NZ,)),
@@ -601,7 +627,7 @@
             dma((2, 4)), dma((2, 4)), dma((2, NY - 1)), dma((2, NY - 1)),
             dma((2, 2, 3)), dma((2, 2, 3)),
             dma((2, 6)), dma((2, 6)), dma((2, NY - 1)), dma((2, NY - 1)),
-            dma((1,)), dma((1,)), dma((NX, 2)), dma((NX,)), pltpu.SemaphoreType.REGULAR,
+            dma((2,)), dma((2,)), dma((NX, 2)), dma((NX,)), pltpu.SemaphoreType.REGULAR,
         ],
         compiler_params=pltpu.CompilerParams(
             collective_id=0, has_side_effects=True, vmem_limit_bytes=56 * 1024 * 1024

time: 115 us -> 112 us (0.974)
  Pallas kernels: 114 us -> 111 us
    pallas_call x1, Pallas kernels: 112 us -> 109 us  [shards(): pl.pallas_call(kernel, out_shape=outs, in_specs=[hbm, hbm, vmem, vmem] +...]
where the time goes in v5:
time: 112 us
  Pallas kernels  111 us (99%)
    pallas_call x1, Pallas kernels, shards(): pl.pallas_call(kernel, out_shape=outs, in_specs=[hbm, hbm, vmem, vmem] +...  109 us

profile of v5, /device:TPU:1, one launch (start us, length us, event | category | flops | bytes accessed | tf_op | source)
XLA Modules:
  0.0 111.5 jit_solution(12871383243705368996)
XLA Ops:
  0.6 108.7 %shard_map.147 = (bf16[128,2048]{1,0:T(8,128)(2,1)}, bf16[128,2048]{1,0:T(8,128)(2,1)}, f32[1,128]{1,0:T(1,128)}, f32[6,1,2048]{2,1,0:T(1,128)}) custom-call(bf16[128,2048]{1,0:T(8,128)(2,1)} %x_hbm.1, bf16[128,2048]{1,0:T(8,128)(2,1)} %cot_hbm.1, s32[1,128]{1,0:T(1,128)} %bitcast.11, f32[1,128]{1,0:T(1,128)} %bitcast.12, bf16[2048,384]{1,0:T(8,128)(2,1)} %bitcast.7, ...), custom_call_target="tpu_custom_call" | custom-call | flops 6000000000 | bytes 16000000 | tf_op jit(solution)/shard_map/pallas_call | solution.py:602
  109.3 2.2 %shard_map.148 = (bf16[128,2048]{1,0:T(8,128)(2,1)}, bf16[128,2048]{1,0:T(8,128)(2,1)}, f32[1,128]{1,0:T(1,128)}, f32[6,1,2048]{2,1,0:T(1,128)}) custom-call(bf16[128,2048]{1,0:T(8,128)(2,1)} %get-tuple-element.12.refs_0_, bf16[128,2048]{1,0:T(8,128)(2,1)} %get-tuple-element.13.refs_1_, f32[1,128]{1,0:T(1,128)} %get-tuple-element.14.refs_2_, ...), custom_call_target="tpu_custom_call" | custom-call | bytes 2200000 | tf_op jit(solution)/shard_map/pallas_call | solution.py:643

commit v6 on v5

--- a/solution.py
+++ b/solution.py
@@ -42,11 +42,12 @@
 def kernel(
     x_hbm, cot_hbm, ids_row, gw_row, wg_hbm, wu_hbm, wd_hbm, pf_hbm, pft_hbm, pn_hbm, pnt_hbm,
     wantc,
-    out_ref, tgrad_ref, ggrad_ref, dgrad_ref,
+    out_hbm, tgrad_hbm, ggrad_hbm, dgrad_hbm,
     x, cot, z, wg, wu, wd, pf, pft, pn, pnt, send, recv, xf, yf, xn, yn, rsend, rrecv,
     oacc, dw, dwb, opp, pure, msend, mrecv, ysum, yb, yrecv, zsend, zrecv, fsend, frecv,
     loc_sem, s1, r1, s2, r2, wzs, wzr, gxs, gxr, gys, gyr, uys, uyr, uxs, uxr,
-    dxs, dxr, dys, dyr, dzs, dzr, fs, fr, go_sem,
+    dxs, dxr, dys, dyr, dzs, dzr, fs, fr, go_sem, out_ref, tgrad_ref, ggrad_ref, dgrad_ref,
+    res_sem,
 ):
     rep = lax.axis_index("rep")
     pz = lax.axis_index("ep")
@@ -143,6 +144,23 @@
         )
 
     place_far = placing(0, FAR)
+    for c in loads[:2]:
+        c.wait()
+    z[0:TOK, :] = x[:, :HALF]
+    z[TOK : 2 * TOK, :] = x[:, HALF:]
+    dout = (gw_c * cot[...].astype(F32)).astype(BF16)
+    z[2 * TOK : 3 * TOK, :] = dout[:, :HALF]
+    z[3 * TOK :, :] = dout[:, HALF:]
+
+    def build(place, first, count):
+        @pl.loop(0, 4)
+        def _(n):
+            cols = ds(n * 256, 256)
+            send[first : first + count, :, cols] = (
+                dot(place, z[:, cols]).astype(BF16).reshape(count, BLK, 256)
+            )
+
+    build(place_far, 0, FAR)
     pl.semaphore_wait(barrier, len(peers))
 
     own = (
@@ -159,24 +177,6 @@
     def _():
         for m in (1, 2, 0):
             wz[m].start()
-
-    for c in loads[:2]:
-        c.wait()
-    z[0:TOK, :] = x[:, :HALF]
-    z[TOK : 2 * TOK, :] = x[:, HALF:]
-    dout = (gw_c * cot[...].astype(F32)).astype(BF16)
-    z[2 * TOK : 3 * TOK, :] = dout[:, :HALF]
-    z[3 * TOK :, :] = dout[:, HALF:]
-
-    def build(place, first, count):
-        @pl.loop(0, 4)
-        def _(n):
-            cols = ds(n * 256, 256)
-            send[first : first + count, :, cols] = (
-                dot(place, z[:, cols]).astype(BF16).reshape(count, BLK, 256)
-            )
-
-    build(place_far, 0, FAR)
 
     def as_source():
         far = [(tie, core, 1, 4 + core), (tie, other, 4, 4 + core)]
@@ -535,6 +535,15 @@
             gsum = gsum + jnp.sum(cot[:, full].astype(F32) * o, axis=1, keepdims=True)
             tgrad_ref[:, full] = (oacc[2 + q, :, cols] + dot(takes[2 + q], src)).astype(BF16)
     ggrad_ref[...] = jnp.sum(jnp.where(eye, gsum, 0.0), axis=0, keepdims=True)
+    gone = [
+        pltpu.make_async_copy(s, d, res_sem.at[i])
+        for i, (s, d) in enumerate(
+            ((out_ref, out_hbm), (tgrad_ref, tgrad_hbm), (ggrad_ref, ggrad_hbm),
+             (dgrad_ref, dgrad_hbm))
+        )
+    ]
+    for c in gone[:3]:
+        c.start()
 
     @pl.when(core == 0)
     def _():
@@ -557,15 +566,36 @@
     for j in range(NX):
         for i in range(6):
             dgrad_ref[i, :, j * QCOL : (j + 1) * QCOL] = frecv[j, i : i + 1, :]
+    gone[3].start()
 
     for c in outs + backs + dx_copies + merged + dy_copies:
         c.wait_send()
+    for c in gone:
+        c.wait()
 
 
 def hand_over(*refs):
-    n = len(refs) // 2
-    for i in range(n):
-        refs[n + i][...] = refs[i][...]
+    src, dst, held, (into, out) = refs[:4], refs[4:8], refs[8:12], refs[12:]
+    parts = []
+    for i in range(2):
+        for r in range(2):
+            parts.append((i, pl.ds(r * (TOK // 2), TOK // 2)))
+    parts += [(2, ALL), (3, ALL)]
+    ins = [
+        pltpu.make_async_copy(src[i].at[r], held[i].at[r], into.at[n])
+        for n, (i, r) in enumerate(parts)
+    ]
+    outs = [
+        pltpu.make_async_copy(held[i].at[r], dst[i].at[r], out.at[n])
+        for n, (i, r) in enumerate(parts)
+    ]
+    for c in ins:
+        c.start()
+    for c, d in zip(ins, outs):
+        c.wait()
+        d.start()
+    for d in outs:
+        d.wait()
 
 
 def gathering(count, pad):
@@ -603,7 +633,7 @@
         kernel,
         out_shape=outs,
         in_specs=[hbm, hbm, vmem, vmem] + [hbm] * 7 + [vmem],
-        out_specs=(vmem,) * 4,
+        out_specs=(hbm,) * 4,
         scratch_shapes=[
             mem((TOK, WIDTH), BF16), mem((TOK, WIDTH), BF16), mem((4 * TOK, HALF), BF16),
             mem((WIDTH, FFW), BF16), mem((WIDTH, FFW), BF16), mem((FFW, WIDTH), BF16),
@@ -628,6 +658,7 @@
             dma((2, 2, 3)), dma((2, 2, 3)),
             dma((2, 6)), dma((2, 6)), dma((2, NY - 1)), dma((2, NY - 1)),
             dma((2,)), dma((2,)), dma((NX, 2)), dma((NX,)), pltpu.SemaphoreType.REGULAR,
+            *[mem(o.shape, o.dtype) for o in outs], dma((4,)),
         ],
         compiler_params=pltpu.CompilerParams(
             collective_id=0, has_side_effects=True, vmem_limit_bytes=56 * 1024 * 1024
@@ -643,8 +674,9 @@
     out, tgrad, ggrad, dgrad = pl.pallas_call(
         hand_over,
         out_shape=outs,
-        in_specs=[vmem] * 4,
-        out_specs=(vmem,) * 4,
+        in_specs=[hbm] * 4,
+        out_specs=(hbm,) * 4,
+        scratch_shapes=[mem(o.shape, o.dtype) for o in outs] + [dma((6,)), dma((6,))],
         cost_estimate=pl.CostEstimate(flops=0, bytes_accessed=2_200_000, transcendentals=0),
     )(*results)
     return out, tgrad, ggrad.reshape(TOK, 1), jnp.transpose(dgrad, (1, 0, 2))

time: 112 us -> 112 us (level)
  no operation moved by 1% of the time
where the time goes in v6:
time: 112 us
  Pallas kernels  111 us (99%)
    pallas_call x1, Pallas kernels, shards(): pl.pallas_call(kernel, out_shape=outs, in_specs=[hbm, hbm, vmem, vmem] +...  109 us

profile of v6, /device:TPU:1, one launch (start us, length us, event | category | flops | bytes accessed | tf_op | source)
XLA Modules:
  0.0 111.8 jit_solution(7732534703022491521)
XLA Ops:
  0.6 109.1 %shard_map.147 = (bf16[128,2048]{1,0:T(8,128)(2,1)}, bf16[128,2048]{1,0:T(8,128)(2,1)}, f32[1,128]{1,0:T(1,128)}, f32[6,1,2048]{2,1,0:T(1,128)}) custom-call(bf16[128,2048]{1,0:T(8,128)(2,1)} %x_hbm.1, bf16[128,2048]{1,0:T(8,128)(2,1)} %cot_hbm.1, s32[1,128]{1,0:T(1,128)} %bitcast.11, f32[1,128]{1,0:T(1,128)} %bitcast.12, bf16[2048,384]{1,0:T(8,128)(2,1)} %bitcast.7, ...), custom_call_target="tpu_custom_call" | custom-call | flops 6000000000 | bytes 16000000 | tf_op jit(solution)/shard_map/pallas_call | solution.py:632
  109.8 2.0 %shard_map.148 = (bf16[128,2048]{1,0:T(8,128)(2,1)}, bf16[128,2048]{1,0:T(8,128)(2,1)}, f32[1,128]{1,0:T(1,128)}, f32[6,1,2048]{2,1,0:T(1,128)}) custom-call(bf16[128,2048]{1,0:T(8,128)(2,1)} %get-tuple-element.12.refs_0_, bf16[128,2048]{1,0:T(8,128)(2,1)} %get-tuple-element.13.refs_1_, f32[1,128]{1,0:T(1,128)} %get-tuple-element.14.refs_2_, ...), custom_call_target="tpu_custom_call" | custom-call | bytes 2200000 | tf_op jit(solution)/shard_map/pallas_call | solution.py:674

commit v7 on v6

--- a/solution.py
+++ b/solution.py
@@ -422,10 +422,6 @@
 
     backs += [back(*e, whence(e)) for e in exp_far]
     results(FAR, NEAR, NPAD, pnt, yn, hf, da, db)
-    for e in exp_near[0:3:2]:
-        c = back(*e, whence(e))
-        c.start()
-        backs.append(c)
     self_back = pltpu.make_async_copy(rsend.at[mine_k], rrecv.at[mine_q], loc_sem.at[10])
     self_back.start()
 
@@ -458,6 +454,10 @@
                        dyr.at[g, k - 1], at_y(k))
             c.start()
             dy_copies.append(c)
+    for e in exp_near[0:3:2]:
+        c = back(*e, whence(e))
+        c.start()
+        backs.append(c)
     sums, dz = [], []
     for g in range(2):
         for c in dy_copies[g * (NY - 1) : (g + 1) * (NY - 1)]:

time: 112 us -> 112 us (level)
  no operation moved by 1% of the time
where the time goes in v7:
time: 112 us
  Pallas kernels  111 us (99%)
    pallas_call x1, Pallas kernels, shards(): pl.pallas_call(kernel, out_shape=outs, in_specs=[hbm, hbm, vmem, vmem] +...  109 us

profile of v7, /device:TPU:1, one launch (start us, length us, event | category | flops | bytes accessed | tf_op | source)
XLA Modules:
  0.0 111.8 jit_solution(13678051942581215896)
XLA Ops:
  0.6 109.1 %shard_map.147 = (bf16[128,2048]{1,0:T(8,128)(2,1)}, bf16[128,2048]{1,0:T(8,128)(2,1)}, f32[1,128]{1,0:T(1,128)}, f32[6,1,2048]{2,1,0:T(1,128)}) custom-call(bf16[128,2048]{1,0:T(8,128)(2,1)} %x_hbm.1, bf16[128,2048]{1,0:T(8,128)(2,1)} %cot_hbm.1, s32[1,128]{1,0:T(1,128)} %bitcast.11, f32[1,128]{1,0:T(1,128)} %bitcast.12, bf16[2048,384]{1,0:T(8,128)(2,1)} %bitcast.7, ...), custom_call_target="tpu_custom_call" | custom-call | flops 6000000000 | bytes 16000000 | tf_op jit(solution)/shard_map/pallas_call | solution.py:632
  109.8 2.0 %shard_map.148 = (bf16[128,2048]{1,0:T(8,128)(2,1)}, bf16[128,2048]{1,0:T(8,128)(2,1)}, f32[1,128]{1,0:T(1,128)}, f32[6,1,2048]{2,1,0:T(1,128)}) custom-call(bf16[128,2048]{1,0:T(8,128)(2,1)} %get-tuple-element.12.refs_0_, bf16[128,2048]{1,0:T(8,128)(2,1)} %get-tuple-element.13.refs_1_, f32[1,128]{1,0:T(1,128)} %get-tuple-element.14.refs_2_, ...), custom_call_target="tpu_custom_call" | custom-call | bytes 2200000 | tf_op jit(solution)/shard_map/pallas_call | solution.py:674
